TPU v7x, 256 devices: a whole 4x4x8 slice. The times are simulated.
256 devices in a mesh: member: 8 (over y, core), rows: 32 (over z, x).
Axes of the slice: x: 4, y: 4, z: 8, core: 2. Of those that a mesh axis runs over, the one named last changes fastest.
Arguments:
- processed_latent_nodes: bfloat16 [8, 16384, 1024], P('member', 'rows'), may hold values from -6 to 6
- grid_embed: bfloat16 [49152, 1024], P('rows'), may hold values from -6 to 6
- dispatch_node_lookup: int32 [1024, 128], P('rows'), may hold values from 0 to 511
- send_count: int32 [1024], P('rows'), may hold values from 1 to 128, as said below
- edge_slot: int32 [3, 49152], P(None, 'rows'), may hold values from 0 to 4095, as said below
- row_points: int32 [32], P('rows'), may hold values from 384 to 1536, as said below
- w_src: bfloat16 [1024, 1024], replicated, may hold values from -0.1875 to 0.1875
- w_dst: bfloat16 [1024, 1024], replicated, may hold values from -0.1875 to 0.1875
- gain_node: float32 [1024], replicated, may hold values from 0.1 to 1.9
- w_node: bfloat16 [1024, 1024], replicated, may hold values from -0.1875 to 0.1875
- w_out: bfloat16 [100, 1024], replicated, may hold values from -0.1875 to 0.1875
- targets: float32 [100, 49152], P(None, 'rows'), may hold values from -6 to 6
- channel_weight: float32 [100], replicated, may hold values from 0.25 to 4
Outputs:
- realization_fields_out: bfloat16 [8, 100, 49152], P('member', None, 'rows')
- score_slope_array: float32 [8, 100, 49152], P('member', None, 'rows')
Inputs may be any that keep to these rules, and one draw needn't show every extreme that they name: `send_count`: slots sent from one shard to one owner; every shard sends all 128 to some owner and one slot to another. `edge_slot`: each edge reads a live slot: c is below send_count of sender s to the point's owner. `row_points`: some slab is full and some holds a quarter of its slots.
All inputs are finite; a program needn't handle non-finite values.
Results may differ from a plain program's by a relative error of at most 0.006.
Values may be sent and summed in bfloat16 or wider, within the bound.
A program may use at most 128 MiB of HBM per device.

v0:
```python
import jax
import jax.numpy as jnp
from jax import lax
from jax.sharding import PartitionSpec as P

SOFT_SCALE = 0.5
EPSILON = 1e-05


def shifted(x, axis, by):
    size = lax.axis_size(axis)
    return lax.ppermute(x, axis, [(i, (i + by) % size) for i in range(size)])


def soft_slope(grid_point_entries):
    return grid_point_entries / jnp.sqrt(
        grid_point_entries * grid_point_entries + SOFT_SCALE * SOFT_SCALE
    )


def local(
    processed_latent_nodes,
    grid_embed,
    dispatch_node_lookup,
    send_count,
    edge_slot,
    row_points,
    w_src,
    w_dst,
    gain_node,
    w_node,
    w_out,
    targets,
    channel_weight,
):
    owners = lax.axis_size("rows")
    capacity = dispatch_node_lookup.shape[1]
    latent_breadth = w_src.shape[1]
    live_slot = jnp.arange(capacity, dtype=jnp.int32)[None, :] < send_count[:, None]
    realization_lines = processed_latent_nodes[0]
    projected = jnp.dot(realization_lines, w_src, preferred_element_type=jnp.float32).astype(
        jnp.bfloat16
    )
    outgoing = jnp.where(
        live_slot[:, :, None], projected[dispatch_node_lookup], jnp.zeros((), jnp.bfloat16)
    )
    received = lax.all_to_all(outgoing, "rows", split_axis=0, concat_axis=0, tiled=True)
    table = received.reshape(owners * capacity, latent_breadth)
    grid_side = jnp.dot(grid_embed, w_dst, preferred_element_type=jnp.float32)
    summed = jnp.zeros(grid_side.shape, jnp.float32)
    for which in range(edge_slot.shape[0]):
        summed = summed + jax.nn.silu(table[edge_slot[which]].astype(jnp.float32) + grid_side)
    scale = lax.rsqrt(jnp.mean(summed * summed, axis=-1, keepdims=True) + EPSILON)
    normed = (summed * scale * gain_node[None, :]).astype(jnp.bfloat16)
    hidden = jax.nn.silu(jnp.dot(normed, w_node, preferred_element_type=jnp.float32)).astype(
        jnp.bfloat16
    )
    expanded_fields = lax.dot_general(
        w_out, hidden, (((1,), (1,)), ((), ())), preferred_element_type=jnp.float32
    )
    exists_indicator = jnp.arange(grid_embed.shape[0], dtype=jnp.int32) < row_points[0]
    realization_fields_out = jnp.where(exists_indicator[None, :], expanded_fields, 0.0).astype(
        jnp.bfloat16
    )
    shard_grid_entries = realization_fields_out.astype(jnp.float32)
    members = lax.axis_size("member")
    pair_sum = jnp.zeros(shard_grid_entries.shape, jnp.float32)
    neighbour_aggregation = realization_fields_out
    for repeat in range(members - 1):
        neighbour_aggregation = shifted(neighbour_aggregation, "member", 1)
        pair_sum = pair_sum + soft_slope(
            shard_grid_entries - neighbour_aggregation.astype(jnp.float32)
        )
    slope_sum = soft_slope(shard_grid_entries - targets) - pair_sum / (members - 1)
    sample_slope_entries = jnp.where(
        exists_indicator[None, :], channel_weight[:, None] * slope_sum, 0.0
    )
    return (realization_fields_out[None], sample_slope_entries[None])


def solution(mesh):
    placed = (
        P("member", "rows", None),
        P("rows", None),
        P("rows", None),
        P("rows"),
        P(None, "rows"),
        P("rows"),
        P(),
        P(),
        P(),
        P(),
        P(),
        P(None, "rows"),
        P(),
    )
    return jax.shard_map(
        local,
        mesh=mesh,
        in_specs=placed,
        out_specs=(P("member", None, "rows"), P("member", None, "rows")),
        check_vma=False,
    )
```

profile of v0, /device:TPU:102, one launch (start us, length us, event | category | flops | bytes accessed | tf_op | source)
XLA Modules:
  0.0 371.7 jit_solution(17519794447102857805)
XLA Ops:
  0.6 0.0 copy-start
  0.6 0.9 fusion.8
  1.5 0.8 iota_compare_fusion
  2.3 4.2 %convolution_convert_fusion = bf16[512,1024]{1,0:T(8,128)(2,1)} fusion(bf16[1024,1024]{1,0:T(8,128)(2,1)} %param.19, bf16[1,512,1024]{2,1,0:T(8,128)(2,1)} %param.13), kind=kOutput, calls=%fused_computation.23 | convolution fusion | flops 1074266112 | bytes 4194304 | tf_op jit(solution)/shard_map/dot_general | solution.py:41
  6.5 22.2 %gather_fusion = bf16[4096,1024]{1,0:T(8,128)(2,1)} fusion(bf16[512,1024]{1,0:T(8,128)(2,1)} %convolution_convert_fusion, s32[4096]{0:T(1024)S(1)} %fusion.8), kind=kCustom, calls=%fused_computation | custom fusion | bytes 16793600 | tf_op jit(solution)/shard_map/gather | solution.py:45
  28.7 7.2 %broadcast_select_fusion = bf16[32,128,1024]{2,1,0:T(8,128)(2,1)} fusion(bf16[32,128,1024]{2,1,0:T(8,128)(2,1)} %bitcast.28, pred[32,128]{1,0:T(8,128)(4,1)S(1)} %iota_compare_fusion), kind=kLoop, calls=%fused_computation.4 | loop fusion | flops 4194304 | bytes 16781312 | tf_op jit(solution)/shard_map/jit(_where)/select_n | solution.py:44
  35.9 0.0 copy-start.2
  35.9 10.4 %all-to-all-start = ((bf16[32,128,1024]{2,1,0:T(8,128)(2,1)}), bf16[32,128,1024]{2,1,0:T(8,128)(2,1)}, u32[]{:S(2)}, u32[]{:S(2)}) async-start(bf16[32,128,1024]{2,1,0:T(8,128)(2,1)} %broadcast_select_fusion), calls=%async_computation | async-start | bytes 16777216 | tf_op jit(solution)/shard_map/all_to_all | solution.py:47
  47.0 0.0 copy-done.2
  47.0 0.1 fusion.9
  47.1 195.4 %all-to-all-done = bf16[32,128,1024]{2,1,0:T(8,128)(2,1)} async-done(((bf16[32,128,1024]{2,1,0:T(8,128)(2,1)}), bf16[32,128,1024]{2,1,0:T(8,128)(2,1)}, u32[]{:S(2)}, u32[]{:S(2)}) %all-to-all-start) | async-done | bytes 8388640 | tf_op jit(solution)/shard_map/all_to_all | solution.py:47
  242.5 12.2 %gather_fusion.2 = bf16[1536,1024]{1,0:T(8,128)(2,1)} fusion(bf16[4096,1024]{1,0:T(8,128)(2,1)} %bitcast.4, s32[2048]{0:T(1024)S(1)} %get-tuple-element.12), kind=kCustom, calls=%fused_computation.2 | custom fusion | bytes 6297600 | tf_op jit(solution)/shard_map/gather | solution.py:52
  254.7 4.7 %copy.22 = bf16[1536,1024]{0,1:T(8,128)(2,1)} copy(bf16[1536,1024]{1,0:T(8,128)(2,1)} %gather_fusion.2) | data formatting | bytes 6291456 | tf_op jit(solution)/shard_map/gather | solution.py:52
  259.4 12.2 %gather_fusion.3 = bf16[1536,1024]{1,0:T(8,128)(2,1)} fusion(bf16[4096,1024]{1,0:T(8,128)(2,1)} %bitcast.4, s32[2048]{0:T(1024)S(1)} %get-tuple-element.11), kind=kCustom, calls=%fused_computation.3 | custom fusion | bytes 6297600 | tf_op jit(solution)/shard_map/gather | solution.py:52
  271.6 4.6 %copy.23 = bf16[1536,1024]{0,1:T(8,128)(2,1)} copy(bf16[1536,1024]{1,0:T(8,128)(2,1)} %gather_fusion.3) | data formatting | bytes 6291456 | tf_op jit(solution)/shard_map/gather | solution.py:52
  276.3 12.2 %gather_fusion.1 = bf16[1536,1024]{1,0:T(8,128)(2,1)} fusion(bf16[4096,1024]{1,0:T(8,128)(2,1)} %bitcast.4, s32[2048]{0:T(1024)S(1)} %pad_clamp_fusion.2), kind=kCustom, calls=%fused_computation.1 | custom fusion | bytes 6297600 | tf_op jit(solution)/shard_map/gather | solution.py:52
  288.5 4.6 %copy.21 = bf16[1536,1024]{0,1:T(8,128)(2,1)} copy(bf16[1536,1024]{1,0:T(8,128)(2,1)} %gather_fusion.1) | data formatting | bytes 6291456 | tf_op jit(solution)/shard_map/gather | solution.py:52
  293.1 0.0 copy-done
  293.1 0.0 copy-start.4
  293.2 12.7 %multiply_reduce_fusion = (f32[1536]{0:T(1024)S(1)}, f32[1536,1024]{0,1:T(8,128)}) fusion(bf16[1536,1024]{0,1:T(8,128)(2,1)} %copy.23, bf16[1536,1024]{0,1:T(8,128)(2,1)} %copy.22, bf16[1536,1024]{0,1:T(8,128)(2,1)} %copy.21, bf16[1536,1024]{1,0:T(8,128)(2,1)S(1)} %copy-done, bf16[1024,1024]{1,0:T(8,128)(2,1)} %param.20), kind=kOutput, calls=%fused_computation.7 | convolution fusion | flops 3255826944 | bytes 20977664 | tf_op jit(solution)/shard_map/dot_general | solution.py:49
  305.9 0.0 copy-done.4
  305.9 0.0 copy-start.3
  305.9 8.7 %fusion.5 = bf16[1536,100]{0,1:T(8,128)(2,1)S(1)} fusion(bf16[100,1024]{1,0:T(8,128)(2,1)} %param.23, bf16[1024,1024]{1,0:T(8,128)(2,1)} %param.22, f32[1536,1024]{0,1:T(8,128)} %get-tuple-element.10, f32[1024]{0:T(1024)S(1)} %copy-done.4, f32[1536]{0:T(1024)S(1)} %add_rsqrt_fusion, pred[1536]{0:T(1024)(128)(4,1)S(1)} %iota_compare_fusion.1), kind=kOutput, calls=%fused_computation.14 | convolution fusion | flops 3548688384 | bytes 8912384 | tf_op jit(solution)/shard_map/dot_general | solution.py:58
  314.6 0.0 copy-start.1
  314.6 0.0 collective-permute-start
  314.6 7.6 %collective-permute-done = bf16[100,1536]{1,0:T(8,128)(2,1)S(1)} collective-permute-done((bf16[100,1536]{1,0:T(8,128)(2,1)S(1)}, bf16[100,1536]{1,0:T(8,128)(2,1)S(1)}, u32[]{:S(2)}, u32[]{:S(2)}) %collective-permute-start) | collective-permute-done | bytes 307232 | tf_op jit(solution)/shard_map/ppermute | solution.py:12
  322.2 0.0 collective-permute-start.1
  322.2 7.6 %collective-permute-done.1 = bf16[100,1536]{1,0:T(8,128)(2,1)S(1)} collective-permute-done((bf16[100,1536]{1,0:T(8,128)(2,1)S(1)}, bf16[100,1536]{1,0:T(8,128)(2,1)S(1)}, u32[]{:S(2)}, u32[]{:S(2)}) %collective-permute-start.1) | collective-permute-done | bytes 307232 | tf_op jit(solution)/shard_map/ppermute | solution.py:12
  329.8 0.0 collective-permute-start.2
  329.8 7.6 %collective-permute-done.2 = bf16[100,1536]{1,0:T(8,128)(2,1)S(1)} collective-permute-done((bf16[100,1536]{1,0:T(8,128)(2,1)S(1)}, bf16[100,1536]{1,0:T(8,128)(2,1)S(1)}, u32[]{:S(2)}, u32[]{:S(2)}) %collective-permute-start.2) | collective-permute-done | bytes 307232 | tf_op jit(solution)/shard_map/ppermute | solution.py:12
  337.4 0.0 collective-permute-start.3
  337.4 7.6 %collective-permute-done.3 = bf16[100,1536]{1,0:T(8,128)(2,1)S(1)} collective-permute-done((bf16[100,1536]{1,0:T(8,128)(2,1)S(1)}, bf16[100,1536]{1,0:T(8,128)(2,1)S(1)}, u32[]{:S(2)}, u32[]{:S(2)}) %collective-permute-start.3) | collective-permute-done | bytes 307232 | tf_op jit(solution)/shard_map/ppermute | solution.py:12
  345.1 0.0 collective-permute-start.4
  345.1 7.6 %collective-permute-done.4 = bf16[100,1536]{1,0:T(8,128)(2,1)S(1)} collective-permute-done((bf16[100,1536]{1,0:T(8,128)(2,1)S(1)}, bf16[100,1536]{1,0:T(8,128)(2,1)S(1)}, u32[]{:S(2)}, u32[]{:S(2)}) %collective-permute-start.4) | collective-permute-done | bytes 307232 | tf_op jit(solution)/shard_map/ppermute | solution.py:12
  352.7 0.0 collective-permute-start.5
  352.7 7.6 %collective-permute-done.5 = bf16[100,1536]{1,0:T(8,128)(2,1)S(1)} collective-permute-done((bf16[100,1536]{1,0:T(8,128)(2,1)S(1)}, bf16[100,1536]{1,0:T(8,128)(2,1)S(1)}, u32[]{:S(2)}, u32[]{:S(2)}) %collective-permute-start.5) | collective-permute-done | bytes 307232 | tf_op jit(solution)/shard_map/ppermute | solution.py:12
  360.3 0.0 collective-permute-start.6
  360.3 7.6 %collective-permute-done.6 = bf16[100,1536]{1,0:T(8,128)(2,1)S(1)} collective-permute-done((bf16[100,1536]{1,0:T(8,128)(2,1)S(1)}, bf16[100,1536]{1,0:T(8,128)(2,1)S(1)}, u32[]{:S(2)}, u32[]{:S(2)}) %collective-permute-start.6) | collective-permute-done | bytes 307232 | tf_op jit(solution)/shard_map/ppermute | solution.py:12
  367.9 0.0 copy-done.3
  367.9 2.3 select_bitcast_fusion
  370.2 1.5 copy.26
  371.7 0.0 copy-done.1
  (4 shorter events, 0.0 us)
Async XLA Ops:
  0.6 292.5 %copy-start = (bf16[1536,1024]{1,0:T(8,128)(2,1)S(1)}, bf16[1536,1024]{1,0:T(8,128)(2,1)}, u32[]{:S(2)}) copy-start(bf16[1536,1024]{1,0:T(8,128)(2,1)} %param.14) | copy-start | bytes 9437188
  35.9 11.1 %copy-start.2 = (s32[3,1536]{1,0:T(4,128)S(1)}, s32[3,1536]{1,0:T(4,128)}, u32[]{:S(2)}) copy-start(s32[3,1536]{1,0:T(4,128)} %param.17) | copy-start | bytes 55300
  35.9 206.6 %all-to-all-start = ((bf16[32,128,1024]{2,1,0:T(8,128)(2,1)}), bf16[32,128,1024]{2,1,0:T(8,128)(2,1)}, u32[]{:S(2)}, u32[]{:S(2)}) async-start(bf16[32,128,1024]{2,1,0:T(8,128)(2,1)} %broadcast_select_fusion), calls=%async_computation | async-start | bytes 16777216 | tf_op jit(solution)/shard_map/all_to_all | solution.py:47
  293.1 12.7 %copy-start.4 = (f32[1024]{0:T(1024)S(1)}, f32[1024]{0:T(1024)}, u32[]{:S(2)}) copy-start(f32[1024]{0:T(1024)} %param.21) | copy-start | bytes 12292
  305.9 62.1 %copy-start.3 = (f32[100]{0:T(128)S(1)}, f32[100]{0:T(128)}, u32[]{:S(2)}) copy-start(f32[100]{0:T(128)} %param.25) | copy-start | bytes 1204
  314.6 57.2 %copy-start.1 = (bf16[1536,100]{0,1:T(8,128)(2,1)}, bf16[1536,100]{0,1:T(8,128)(2,1)S(1)}, u32[]{:S(2)}) copy-start(bf16[1536,100]{0,1:T(8,128)(2,1)S(1)} %fusion.5) | copy-start | bytes 921604
  314.6 7.6 %collective-permute-start = (bf16[100,1536]{1,0:T(8,128)(2,1)S(1)}, bf16[100,1536]{1,0:T(8,128)(2,1)S(1)}, u32[]{:S(2)}, u32[]{:S(2)}) collective-permute-start(bf16[100,1536]{1,0:T(8,128)(2,1)S(1)} %bitcast.29), channel_id=1, source_target_pairs={{0,32},{32,64},{64,96},{96,128},{128,160},{160,192},{192,224},{224... | collective-permute-start | bytes 921608 | tf_op jit(solution)/shard_map/ppermute | solution.py:12
  322.2 7.6 %collective-permute-start.1 = (bf16[100,1536]{1,0:T(8,128)(2,1)S(1)}, bf16[100,1536]{1,0:T(8,128)(2,1)S(1)}, u32[]{:S(2)}, u32[]{:S(2)}) collective-permute-start(bf16[100,1536]{1,0:T(8,128)(2,1)S(1)} %collective-permute-done), channel_id=1, source_target_pairs={{0,32},{32,64},{64,96},{96,128},{128,160},{160,192},{192,224},{224... | collective-permute-start | bytes 921608 | tf_op jit(solution)/shard_map/ppermute | solution.py:12
  329.8 7.6 %collective-permute-start.2 = (bf16[100,1536]{1,0:T(8,128)(2,1)S(1)}, bf16[100,1536]{1,0:T(8,128)(2,1)S(1)}, u32[]{:S(2)}, u32[]{:S(2)}) collective-permute-start(bf16[100,1536]{1,0:T(8,128)(2,1)S(1)} %collective-permute-done.1), channel_id=1, source_target_pairs={{0,32},{32,64},{64,96},{96,128},{128,160},{160,192},{192,224},{224... | collective-permute-start | bytes 921608 | tf_op jit(solution)/shard_map/ppermute | solution.py:12
  337.4 7.6 %collective-permute-start.3 = (bf16[100,1536]{1,0:T(8,128)(2,1)S(1)}, bf16[100,1536]{1,0:T(8,128)(2,1)S(1)}, u32[]{:S(2)}, u32[]{:S(2)}) collective-permute-start(bf16[100,1536]{1,0:T(8,128)(2,1)S(1)} %collective-permute-done.2), channel_id=1, source_target_pairs={{0,32},{32,64},{64,96},{96,128},{128,160},{160,192},{192,224},{224... | collective-permute-start | bytes 921608 | tf_op jit(solution)/shard_map/ppermute | solution.py:12
  345.1 7.6 %collective-permute-start.4 = (bf16[100,1536]{1,0:T(8,128)(2,1)S(1)}, bf16[100,1536]{1,0:T(8,128)(2,1)S(1)}, u32[]{:S(2)}, u32[]{:S(2)}) collective-permute-start(bf16[100,1536]{1,0:T(8,128)(2,1)S(1)} %collective-permute-done.3), channel_id=1, source_target_pairs={{0,32},{32,64},{64,96},{96,128},{128,160},{160,192},{192,224},{224... | collective-permute-start | bytes 921608 | tf_op jit(solution)/shard_map/ppermute | solution.py:12
  352.7 7.6 %collective-permute-start.5 = (bf16[100,1536]{1,0:T(8,128)(2,1)S(1)}, bf16[100,1536]{1,0:T(8,128)(2,1)S(1)}, u32[]{:S(2)}, u32[]{:S(2)}) collective-permute-start(bf16[100,1536]{1,0:T(8,128)(2,1)S(1)} %collective-permute-done.4), channel_id=1, source_target_pairs={{0,32},{32,64},{64,96},{96,128},{128,160},{160,192},{192,224},{224... | collective-permute-start | bytes 921608 | tf_op jit(solution)/shard_map/ppermute | solution.py:12
  360.3 7.6 %collective-permute-start.6 = (bf16[100,1536]{1,0:T(8,128)(2,1)S(1)}, bf16[100,1536]{1,0:T(8,128)(2,1)S(1)}, u32[]{:S(2)}, u32[]{:S(2)}) collective-permute-start(bf16[100,1536]{1,0:T(8,128)(2,1)S(1)} %collective-permute-done.5), channel_id=1, source_target_pairs={{0,32},{32,64},{64,96},{96,128},{128,160},{160,192},{192,224},{224... | collective-permute-start | bytes 921608 | tf_op jit(solution)/shard_map/ppermute | solution.py:12
where the time goes:
time: 372 us
  waiting for transfers between devices  249 us (67%)
  local copies, waits for them, and re-layouts  74.3 us (20%)
  matrix products  25.6 us (7%)
  other arithmetic  11.3 us (3%)
  starting transfers between devices  10.4 us (3%)
    all_to_all x1, waiting for transfers between devices, local(): lax.all_to_all(outgoing, 'rows', split_axis=0, concat_axis=0, tiled=True)  195 us
    ppermute x7, waiting for transfers between devices, shifted(): return lax.ppermute(x, axis, [(i, (i + by) % size) for i in range(size)])  53.3 us
    gather x6, local copies, waits for them, and re-layouts, local(): table[edge_slot[which]].astype(jnp.float32) + grid_side  50.6 us
    gather x1, local copies, waits for them, and re-layouts, local(): projected[dispatch_node_lookup]  22.2 us
    dot_general x1, matrix products, local(): grid_side = jnp.dot(grid_embed, w_dst, preferred_element_type=jnp.float32)  12.7 us
    all_to_all x1, starting transfers between devices, local(): lax.all_to_all(outgoing, 'rows', split_axis=0, concat_axis=0, tiled=True)  10.4 us
    dot_general x1, matrix products, local(): lax.dot_general(w_out, hidden, (((1,), (1,)), ((), ())), preferred_elemen...  8.66 us
  transfers between devices with their start and end apart: 8, of which 8 were waited for; matrix products, arithmetic and copies ran while one was open for 0% of the time, Pallas kernels for 0%

commit v1 on v0

v1 whole, which is shorter than its diff:
```python
import functools

import jax
import jax.numpy as jnp
from jax import lax
from jax.experimental import pallas as pl
from jax.experimental.pallas import tpu as pltpu
from jax.sharding import PartitionSpec as P

SOFT_SCALE = 0.5
EPSILON = 1e-05
MESH = pl.DeviceIdType.MESH

NZ, NX, NY = 8, 4, 4
ROWS = NZ * NX
MEMBERS = 8
CAP = 128
NODES = 512
D = 1024
W = 512
G = 1536
C = 100
CP = 112
K = 3
PB = 256
MIB = 1 << 20


def row_id(z, x):
    return lax.rem(z, NZ) * NX + lax.rem(x, NX)


def table_kernel(
    latent, w_src, look, embed_hbm, wdst_hbm, tab, gs_out,
    T, stage, fwd_p, fwd_m, L, LC, embed, wdst, gs,
    lk_s, lk_r, z_s, z_r, x_s, x_r, loc, pre,
):
    me = lax.axis_index("rows")
    z = me // NX
    x = lax.rem(me, NX)

    barrier = pltpu.get_barrier_semaphore()
    peers = [row_id(z + k, x) for k in range(1, NZ)]
    peers += [row_id(z, x + 1), row_id(z, x + 3)]
    for peer in peers:
        pl.semaphore_signal(barrier, inc=1, device_id={"rows": peer}, device_id_type=MESH)

    load_embed = pltpu.make_async_copy(embed_hbm, embed, pre.at[0])
    load_wdst = pltpu.make_async_copy(wdst_hbm, wdst, pre.at[1])
    load_embed.start()
    load_wdst.start()

    def project(h):
        @pl.loop(0, NODES // 128)
        def _(i):
            rows = pl.ds(pl.multiple_of(i * 128, 128), 128)
            T[h, z, rows, :] = jnp.dot(
                latent[rows, :], w_src[:, h * W:(h + 1) * W],
                preferred_element_type=jnp.float32,
            ).astype(jnp.bfloat16)

    def remote(src, dst, ss, rs, to):
        return pltpu.make_async_remote_copy(
            src_ref=src, dst_ref=dst, send_sem=ss, recv_sem=rs,
            device_id={"rows": to}, device_id_type=MESH,
        )

    def z_copy(direction, d, h):
        if direction == 0:
            shard, to = lax.rem(z + NZ - (d - 1), NZ), row_id(z + 1, x)
        else:
            shard, to = lax.rem(z + (d - 1), NZ), row_id(z + NZ - 1, x)
        i = (direction * 4 + d - 1) * 2 + h
        return remote(T.at[h, shard], T.at[h, shard], z_s.at[i], z_r.at[i], to)

    def z_arrival(direction, d, h):
        if direction == 0:
            shard = lax.rem(z + NZ - d, NZ)
        else:
            shard = lax.rem(z + d, NZ)
        i = (direction * 4 + d - 1) * 2 + h
        return remote(T.at[h, shard], T.at[h, shard], z_s.at[i], z_r.at[i], row_id(z + 1, x))

    def lk_copy(k):
        to_z = lax.rem(z + k, NZ)
        return remote(look.at[to_z], L.at[z], lk_s.at[k], lk_r.at[z], row_id(to_z, x))

    def lk_arrival(shard):
        return remote(look.at[shard], L.at[shard], lk_s.at[0], lk_r.at[shard], row_id(z + 1, x))

    def x_copies(h, shard, item):
        right, left = row_id(z, x + 1), row_id(z, x + 3)
        own = shard * NX + x
        base = item * 6
        to_right = stage.at[h, shard, lax.rem(x + 1, NX)]
        to_left = stage.at[h, shard, lax.rem(x + 3, NX)]
        far = stage.at[h, shard, lax.rem(x + 2, NX)]
        return [
            remote(far.at[pl.ds(0, 64)], fwd_p.at[h, shard], x_s.at[base + 2], x_r.at[base + 2], right),
            remote(far.at[pl.ds(64, 64)], fwd_m.at[h, shard], x_s.at[base + 3], x_r.at[base + 3], left),
            remote(to_right, tab.at[h, own], x_s.at[base], x_r.at[base], right),
            remote(to_left, tab.at[h, own], x_s.at[base + 1], x_r.at[base + 1], left),
        ]

    def x_forwards(h, shard, item):
        right, left = row_id(z, x + 1), row_id(z, x + 3)
        base = item * 6
        return [
            remote(
                fwd_p.at[h, shard],
                tab.at[h, shard * NX + lax.rem(x + 3, NX), pl.ds(0, 64)],
                x_s.at[base + 4], x_r.at[base + 4], right,
            ),
            remote(
                fwd_m.at[h, shard],
                tab.at[h, shard * NX + lax.rem(x + 1, NX), pl.ds(64, 64)],
                x_s.at[base + 5], x_r.at[base + 5], left,
            ),
        ]

    def x_arrivals(h, shard, item):
        base = item * 6
        to = row_id(z, x + 1)
        far = shard * NX + lax.rem(x + 2, NX)
        spots = [
            tab.at[h, shard * NX + lax.rem(x + 3, NX)],
            tab.at[h, shard * NX + lax.rem(x + 1, NX)],
            fwd_p.at[h, shard],
            fwd_m.at[h, shard],
            tab.at[h, far, pl.ds(0, 64)],
            tab.at[h, far, pl.ds(64, 64)],
        ]
        return [remote(s, s, x_s.at[base + i], x_r.at[base + i], to) for i, s in enumerate(spots)]

    def local_copy(h, shard, item):
        return pltpu.make_async_copy(stage.at[h, shard, x], tab.at[h, shard * NX + x], loc.at[item])

    def columns(shard):
        for r in range(NX):
            line = jnp.broadcast_to(L[shard, r:r + 1, :], (128, 128))
            LC[shard, r] = jnp.transpose(line)

    def select(h, shard):
        @pl.loop(0, NX)
        def _(r):
            col = LC[shard, r]
            lane = lax.broadcasted_iota(jnp.int32, (CAP, 128), 1)
            hot = jnp.concatenate(
                [jnp.where(col == lane + 128 * t, 1.0, 0.0) for t in range(NODES // 128)], axis=1
            ).astype(jnp.bfloat16)
            stage[h, shard, r] = jnp.dot(
                hot, T[h, shard], preferred_element_type=jnp.float32
            ).astype(jnp.bfloat16)

    def launch(h, shard, item):
        select(h, shard)
        for copy in x_copies(h, shard, item):
            copy.start()
        local_copy(h, shard, item).start()

    def forward(h, shard, item):
        arrived = x_arrivals(h, shard, item)
        copies = x_forwards(h, shard, item)
        arrived[2].wait_recv()
        copies[0].start()
        arrived[3].wait_recv()
        copies[1].start()

    project(0)
    pl.semaphore_wait(barrier, len(peers))
    z_copy(0, 1, 0).start()
    z_copy(1, 1, 0).start()
    for k in range(1, NZ):
        lk_copy(k).start()
    project(1)
    z_copy(0, 1, 1).start()
    z_copy(1, 1, 1).start()

    L[z] = look[z]
    columns(z)
    items = []
    for h in range(2):
        items.append((h, z, len(items)))
        launch(*items[-1])

    load_embed.wait()
    load_wdst.wait()

    def grid_side(part):
        @pl.loop(part * 3, part * 3 + 3)
        def _(i):
            rows = pl.ds(pl.multiple_of(i * 128, 128), 128)
            for j in range(4):
                value = jnp.dot(
                    embed[rows, :], wdst[:, j * 256:(j + 1) * 256], preferred_element_type=jnp.float32
                )
                for r in range(16):
                    for t in range(2):
                        gs[pl.ds((i * 128 + r * 8) * 8 + j * 2 + t, 8, stride=8), :] = 0.5 * value[
                            r * 8:(r + 1) * 8, t * 128:(t + 1) * 128
                        ]

    grid_side(0)
    grid_side(1)
    served = 0
    pending = list(items)
    for d in range(1, 4):
        below = lax.rem(z + NZ - d, NZ)
        above = lax.rem(z + d, NZ)
        for h in range(2):
            z_arrival(0, d, h).wait_recv()
            if d < 3 or h == 0:
                z_copy(0, d + 1, h).start()
            z_arrival(1, d, h).wait_recv()
            if d < 3 or h == 1:
                z_copy(1, d + 1, h).start()
            if h == 0:
                for shard in (below, above):
                    lk_arrival(shard).wait_recv()
                    columns(shard)
            for item in pending:
                forward(*item)
            pending = []
            for shard in (below, above):
                items.append((h, shard, len(items)))
                pending.append(items[-1])
                launch(*items[-1])
        if d == 1:
            grid_side(2)
            grid_side(3)
            save_gs = pltpu.make_async_copy(gs, gs_out, pre.at[2])
            save_gs.start()
    last = lax.rem(z + 4, NZ)
    lk_arrival(last).wait_recv()
    columns(last)
    for h in range(2):
        z_arrival(h, 4, h).wait_recv()
        for item in pending:
            forward(*item)
        items.append((h, last, len(items)))
        pending = [items[-1]]
        launch(*items[-1])
    for item in pending:
        forward(*item)

    for item in items:
        arrived = x_arrivals(*item)
        for i in (0, 1, 4, 5):
            arrived[i].wait_recv()
        for copy in x_copies(*item) + x_forwards(*item):
            copy.wait_send()
        local_copy(*item).wait()
    for d in range(1, 5):
        for h in range(2):
            for direction in range(2):
                if d < 4 or h == direction:
                    z_copy(direction, d, h).wait_send()
    for k in range(1, NZ):
        lk_copy(k).wait_send()
    save_gs.wait()


def table_call(latent, w_src, look, embed, w_dst):
    n_items = 2 * NZ
    vm = pl.BlockSpec(memory_space=pltpu.VMEM)
    hbm = pl.BlockSpec(memory_space=pl.ANY)
    dma = pltpu.SemaphoreType.DMA
    return pl.pallas_call(
        table_kernel,
        out_shape=(
            jax.ShapeDtypeStruct((2, ROWS, CAP, W), jnp.bfloat16),
            jax.ShapeDtypeStruct((G * 8, 128), jnp.float32),
        ),
        in_specs=[vm, vm, vm, hbm, hbm],
        out_specs=(hbm, hbm),
        scratch_shapes=[
            pltpu.VMEM((2, NZ, NODES, W), jnp.bfloat16),
            pltpu.VMEM((2, NZ, NX, CAP, W), jnp.bfloat16),
            pltpu.VMEM((2, NZ, 64, W), jnp.bfloat16),
            pltpu.VMEM((2, NZ, 64, W), jnp.bfloat16),
            pltpu.VMEM((NZ, NX, CAP), jnp.int32),
            pltpu.VMEM((NZ, NX, CAP, 128), jnp.int32),
            pltpu.VMEM((G, D), jnp.bfloat16),
            pltpu.VMEM((D, D), jnp.bfloat16),
            pltpu.VMEM((G * 8, 128), jnp.float32),
            dma((NZ,)), dma((NZ,)),
            dma((16,)), dma((16,)),
            dma((n_items * 6,)), dma((n_items * 6,)),
            dma((n_items,)), dma((3,)),
        ],
        compiler_params=pltpu.CompilerParams(
            collective_id=0, has_side_effects=True, vmem_limit_bytes=56 * MIB
        ),
        cost_estimate=pl.CostEstimate(flops=14 * 10**9, bytes_accessed=30 * MIB, transcendentals=0),
        name="table",
    )(latent, w_src, look, embed, w_dst)


def decode_kernel(edge, rp, tab, gs, w_node, w_out, gain, out, F, S):
    @pl.loop(0, ROWS)
    def _(s):
        for r in range(CAP // 16):
            for h in range(2):
                value = tab[h, s, r * 16:(r + 1) * 16, :].astype(jnp.float32) * 0.5
                for u in range(2):
                    for j in range(4):
                        start = (s * CAP + r * 16 + u * 8) * 8 + h * 4 + j
                        F[pl.ds(start, 8, stride=8), :] = value[
                            u * 8:(u + 1) * 8, j * 128:(j + 1) * 128
                        ]

    gain_row = gain[...]

    @pl.loop(0, G // PB)
    def _(b):
        first = b * PB

        @pl.loop(0, PB // 8)
        def _(q):
            for u in range(8):
                p = first + q * 8 + u
                g = gs[pl.ds(pl.multiple_of(p * 8, 8), 8), :]
                total = jnp.zeros((8, 128), jnp.float32)
                for k in range(K):
                    row = pl.multiple_of(edge[k, p] * 8, 8)
                    half = F[pl.ds(row, 8), :] + g
                    total = total + (half + half * jnp.tanh(half))
                S[pl.ds(q * 64 + u, 8, stride=8), :] = total

        cube = S[...].reshape(PB // 8, 8, 8, 128)
        summed = jnp.concatenate([cube[:, j].reshape(PB, 128) for j in range(8)], axis=1)
        scale = lax.rsqrt(jnp.mean(summed * summed, axis=-1, keepdims=True) + EPSILON)
        normed = (summed * scale * gain_row).astype(jnp.bfloat16)
        half = 0.5 * jnp.dot(normed, w_node[...], preferred_element_type=jnp.float32)
        hidden = (half + half * jnp.tanh(half)).astype(jnp.bfloat16)
        fields = lax.dot_general(
            w_out[...], hidden, (((1,), (1,)), ((), ())), preferred_element_type=jnp.float32
        )
        point = lax.broadcasted_iota(jnp.int32, (C, PB), 1) + first
        lanes = pl.ds(pl.multiple_of(lax.rem(b, 3) * PB, 128), PB)
        out[b // 3, 0:C, lanes] = jnp.where(point < rp[0], fields, 0.0).astype(jnp.bfloat16)
        out[b // 3, C:CP, lanes] = jnp.zeros((CP - C, PB), jnp.bfloat16)


def decode_call(edge, rp, tab, gs, w_node, w_out, gain):
    vm = pl.BlockSpec(memory_space=pltpu.VMEM)
    sm = pl.BlockSpec(memory_space=pltpu.SMEM)
    return pl.pallas_call(
        decode_kernel,
        out_shape=jax.ShapeDtypeStruct((2, CP, G // 2), jnp.bfloat16),
        in_specs=[sm, sm, vm, vm, vm, vm, vm],
        out_specs=vm,
        scratch_shapes=[
            pltpu.VMEM((ROWS * CAP * 8, 128), jnp.float32),
            pltpu.VMEM((PB * 8, 128), jnp.float32),
        ],
        compiler_params=pltpu.CompilerParams(vmem_limit_bytes=56 * MIB),
        name="decode",
    )(edge, rp, tab, gs, w_node, w_out, gain)


def score_kernel(rp, mine, targets, weight, fields_out, score_out, X, send, recv):
    m = lax.axis_index("member")
    y = m // 2
    c = lax.rem(m, 2)

    def chip(k):
        return lax.rem(y + k, NY) * 2

    up, down, far, partner = chip(1) + c, chip(3) + c, chip(2) + c, chip(0) + 1 - c
    barrier = pltpu.get_barrier_semaphore()
    for peer in (up, down, partner):
        pl.semaphore_signal(barrier, inc=1, device_id={"member": peer}, device_id_type=MESH)
    pl.semaphore_wait(barrier, 3)

    def remote(src, dst, i, to):
        return pltpu.make_async_remote_copy(
            src_ref=src, dst_ref=dst, send_sem=send.at[i], recv_sem=recv.at[i],
            device_id={"member": to}, device_id_type=MESH,
        )

    own = [
        remote(mine.at[0], X.at[m, 0], 0, up),
        remote(mine.at[1], X.at[m, 1], 1, down),
        remote(mine.at[1], X.at[m, 1], 2, up),
        remote(mine.at[0], X.at[m, 0], 3, down),
        remote(mine, X.at[m], 4, partner),
    ]
    landed = [
        remote(X.at[down, 0], X.at[down, 0], 0, up),
        remote(X.at[up, 1], X.at[up, 1], 1, up),
        remote(X.at[down, 1], X.at[down, 1], 2, up),
        remote(X.at[up, 0], X.at[up, 0], 3, up),
        remote(X.at[partner], X.at[partner], 4, up),
    ]
    passed = [
        remote(X.at[down, 0], X.at[down, 0], 5, up),
        remote(X.at[up, 1], X.at[up, 1], 6, down),
    ]
    passed_landed = [
        remote(X.at[far, 0], X.at[far, 0], 5, up),
        remote(X.at[far, 1], X.at[far, 1], 6, up),
    ]
    o = 1 - 2 * c
    across = [
        remote(X.at[down], X.at[down], 7, partner),
        remote(X.at[up], X.at[up], 8, partner),
        remote(X.at[far], X.at[far], 9, partner),
    ]
    across_landed = [
        remote(X.at[down + o], X.at[down + o], 7, up),
        remote(X.at[up + o], X.at[up + o], 8, up),
        remote(X.at[far + o], X.at[far + o], 9, up),
    ]
    for copy in own:
        copy.start()
    X[m] = mine[...]
    landed[0].wait_recv()
    passed[0].start()
    landed[1].wait_recv()
    passed[1].start()
    landed[2].wait_recv()
    across[0].start()
    landed[3].wait_recv()
    across[1].start()
    passed_landed[0].wait_recv()
    passed_landed[1].wait_recv()
    across[2].start()
    landed[4].wait_recv()
    for copy in across_landed:
        copy.wait_recv()

    def slope(v):
        return v * lax.rsqrt(v * v + SOFT_SCALE * SOFT_SCALE)

    scale = weight[...]

    @pl.loop(0, G // 128)
    def _(t):
        half = t // 6
        lanes = pl.ds(pl.multiple_of(lax.rem(t, 6) * 128, 128), 128)
        whole = pl.ds(pl.multiple_of(t * 128, 128), 128)
        raw = mine[half, 0:C, lanes]
        here = raw.astype(jnp.float32)
        pair = jnp.zeros((C, 128), jnp.float32)
        for j in range(MEMBERS):
            pair = pair + slope(here - X[j, half, 0:C, lanes].astype(jnp.float32))
        total = slope(here - targets[:, whole]) - pair * (1.0 / (MEMBERS - 1))
        point = lax.broadcasted_iota(jnp.int32, (C, 128), 1) + t * 128
        fields_out[:, whole] = raw
        score_out[:, whole] = jnp.where(point < rp[0], scale * total, 0.0)

    for copy in own + passed + across:
        copy.wait_send()


def score_call(rp, mine, targets, weight):
    vm = pl.BlockSpec(memory_space=pltpu.VMEM)
    sm = pl.BlockSpec(memory_space=pltpu.SMEM)
    return pl.pallas_call(
        score_kernel,
        out_shape=(
            jax.ShapeDtypeStruct((C, G), jnp.bfloat16),
            jax.ShapeDtypeStruct((C, G), jnp.float32),
        ),
        in_specs=[sm, vm, vm, vm],
        out_specs=(vm, vm),
        scratch_shapes=[
            pltpu.VMEM((MEMBERS, 2, CP, G // 2), jnp.bfloat16),
            pltpu.SemaphoreType.DMA((10,)),
            pltpu.SemaphoreType.DMA((10,)),
        ],
        compiler_params=pltpu.CompilerParams(
            collective_id=1, has_side_effects=True, vmem_limit_bytes=32 * MIB
        ),
        name="score",
    )(rp, mine, targets, weight)


def local(
    processed_latent_nodes, grid_embed, dispatch_node_lookup, send_count, edge_slot, row_points,
    w_src, w_dst, gain_node, w_node, w_out, targets, channel_weight,
):
    del send_count
    look = dispatch_node_lookup.reshape(NZ, NX, CAP)
    tab, gs = table_call(processed_latent_nodes[0], w_src, look, grid_embed, w_dst)
    mine = decode_call(edge_slot, row_points, tab, gs, w_node, w_out, gain_node[None, :])
    fields, score = score_call(row_points, mine, targets, channel_weight[:, None])
    return fields[None], score[None]


def solution(mesh):
    placed = (
        P("member", "rows", None),
        P("rows", None),
        P("rows", None),
        P("rows"),
        P(None, "rows"),
        P("rows"),
        P(),
        P(),
        P(),
        P(),
        P(),
        P(None, "rows"),
        P(),
    )
    return jax.shard_map(
        local,
        mesh=mesh,
        in_specs=placed,
        out_specs=(P("member", None, "rows"), P("member", None, "rows")),
        check_vma=False,
    )
```

time: 372 us -> 160 us (0.43)
  the two profiles are of different devices: /device:TPU:102 before, /device:TPU:1 now
where the time goes in v1:
time: 160 us
  Pallas kernels  155 us (97%)
  local copies, waits for them, and re-layouts  3.28 us (2%)
    pallas_call x1, Pallas kernels, table_call(): pl.pallas_call(table_kernel, out_shape=(jax.ShapeDtypeStruct((2, ROWS, CA...  109 us
    pallas_call x1, Pallas kernels, decode_call(): pl.pallas_call(decode_kernel, out_shape=jax.ShapeDtypeStruct((2, CP, G //...  26 us
    pallas_call x1, Pallas kernels, score_call(): pl.pallas_call(score_kernel, out_shape=(jax.ShapeDtypeStruct((C, G), jnp....  19.8 us

profile of v1, /device:TPU:1, one launch (start us, length us, event | category | flops | bytes accessed | tf_op | source)
XLA Modules:
  0.0 159.6 jit_solution(8874804488648486057)
XLA Ops:
  0.6 109.2 %table.1 = (bf16[2,32,128,512]{3,2,1,0:T(8,128)(2,1)}, f32[12288,128]{1,0:T(8,128)}) custom-call(bf16[512,1024]{1,0:T(8,128)(2,1)} %bitcast.10, bf16[1024,1024]{1,0:T(8,128)(2,1)} %w_src.1, s32[8,4,128]{2,1,0:T(4,128)} %bitcast.11, bf16[1536,1024]{1,0:T(8,128)(2,1)} %embed_hbm.1, bf16[1024,1024]{1,0:T(8,128)(2,1)} %wdst_hbm.1), custom_call_target="tpu_custom_call" | custom-call | flops 14000000000 | bytes 31457280 | tf_op jit(solution)/shard_map/table/pallas_call | solution.py:268
  110.5 0.0 copy-start.2
  110.5 0.0 copy-start.1
  110.5 26.0 %decode.1.mine = bf16[2,112,768]{2,1,0:T(8,128)(2,1)} custom-call(s32[3,1536]{1,0:T(4,128)} %edge.1, s32[1]{0:T(128)S(6)} %copy.17.rp, bf16[2,32,128,512]{3,2,1,0:T(8,128)(2,1)} %get-tuple-element.6.tab, f32[12288,128]{1,0:T(8,128)} %get-tuple-element.7.gs, bf16[1024,1024]{1,0:T(8,128)(2,1)} %w_node.1, bf16[100,1024]{1,0:T(8,128)(2,1)} %w_out.1, ...), custom_call_target="tpu_custom_call" | custom-call | tf_op jit(solution)/shard_map/decode/pallas_call | solution.py:348
  136.5 0.0 copy-done.2
  136.5 0.1 copy.14.weight
  136.6 0.0 copy-done.1
  136.6 0.0 copy-start
  136.6 1.0 copy-done
  137.6 19.8 %score.1 = (bf16[100,1536]{1,0:T(8,128)(2,1)S(1)}, f32[100,1536]{1,0:T(8,128)S(1)}) custom-call(s32[1]{0:T(128)S(6)} %copy.17.rp, bf16[2,112,768]{2,1,0:T(8,128)(2,1)S(1)} %copy-done, f32[100,1536]{1,0:T(8,128)S(1)} %copy-done.1, f32[100,1]{1,0:T(8,128)S(1)} %copy.14.weight), custom_call_target="tpu_custom_call" | custom-call | tf_op jit(solution)/shard_map/score/pallas_call | solution.py:460
  157.4 1.5 copy.15
  158.9 0.7 copy.18
Async XLA Ops:
  110.5 26.0 %copy-start.2 = (f32[100]{0:T(128)S(1)}, f32[100]{0:T(128)}, u32[]{:S(2)}) copy-start(f32[100]{0:T(128)} %param.24) | copy-start | bytes 1204
  110.5 26.1 %copy-start.1 = (f32[100,1536]{1,0:T(8,128)S(1)}, f32[100,1536]{1,0:T(8,128)}, u32[]{:S(2)}) copy-start(f32[100,1536]{1,0:T(8,128)} %targets.1) | copy-start | bytes 1843204
  136.6 1.0 copy-start

commit v2 on v0

v2 whole, which is shorter than its diff:
```python
import functools

import jax
import jax.numpy as jnp
from jax import lax
from jax.experimental import pallas as pl
from jax.experimental.pallas import tpu as pltpu
from jax.sharding import PartitionSpec as P

SOFT_SCALE = 0.5
EPSILON = 1e-05
MESH = pl.DeviceIdType.MESH

NZ, NX, NY = 8, 4, 4
ROWS = NZ * NX
MEMBERS = 8
CAP = 128
NODES = 512
D = 1024
W = 512
G = 1536
C = 100
CP = 112
K = 3
PB = 256
NB = G // PB
SLOTS = 8
MIB = 1 << 20
VMEM_LIMIT = 63 * MIB


def row_id(z, x):
    return lax.rem(z, NZ) * NX + lax.rem(x, NX)


def decoder_kernel(
    edge, rp, latent, w_src, look, gain, weight,
    embed_hbm, wdst_hbm, wnode_hbm, wout_hbm, targets_hbm,
    fields_out, score_out,
    T, stage, landing, fwd_p, fwd_m, L, LC, F, gs, S, X,
    embed, wdst, w_node, w_out, targets,
    lk_s, lk_r, z_s, z_r, x_s, x_r, m_s, m_r, pre,
):
    me = lax.axis_index("rows")
    z = me // NX
    x = lax.rem(me, NX)
    m = lax.axis_index("member")
    y = m // 2
    c = lax.rem(m, 2)
    right, left = row_id(z, x + 1), row_id(z, x + 3)
    north, south = row_id(z + 1, x), row_id(z + NZ - 1, x)

    flat = F.reshape(ROWS * CAP * 8, 128)

    def chip(k):
        return lax.rem(y + k, NY) * 2

    up, down, far, partner = chip(1) + c, chip(3) + c, chip(2) + c, chip(0) + 1 - c
    other = 1 - 2 * c

    barrier = pltpu.get_barrier_semaphore()
    peers = [{"rows": row_id(z + k, x)} for k in range(1, NZ)]
    peers += [{"rows": right}, {"rows": left}]
    peers += [{"member": up}, {"member": down}, {"member": partner}]
    for peer in peers:
        pl.semaphore_signal(barrier, inc=1, device_id=peer, device_id_type=MESH)

    loads = [
        pltpu.make_async_copy(a, b, pre.at[i])
        for i, (a, b) in enumerate([
            (embed_hbm, embed), (wdst_hbm, wdst), (wnode_hbm, w_node), (wout_hbm, w_out),
            (targets_hbm, targets),
        ])
    ]
    for load in loads:
        load.start()

    def remote(src, dst, ss, rs, **to):
        return pltpu.make_async_remote_copy(
            src_ref=src, dst_ref=dst, send_sem=ss, recv_sem=rs,
            device_id=to, device_id_type=MESH,
        )

    def project(h):
        @pl.loop(0, NODES // 128)
        def _(i):
            rows = pl.ds(pl.multiple_of(i * 128, 128), 128)
            T[h, z, rows, :] = jnp.dot(
                latent[rows, :], w_src[:, h * W:(h + 1) * W],
                preferred_element_type=jnp.float32,
            ).astype(jnp.bfloat16)

    def z_copy(direction, d, h, arriving=False):
        back = d if arriving else d - 1
        shard = lax.rem(z + NZ - back, NZ) if direction == 0 else lax.rem(z + back, NZ)
        i = (direction * 4 + d - 1) * 2 + h
        return remote(
            T.at[h, shard], T.at[h, shard], z_s.at[i], z_r.at[i],
            rows=north if direction == 0 else south,
        )

    def lk_copy(k):
        to_z = lax.rem(z + k, NZ)
        return remote(look.at[to_z], L.at[z], lk_s.at[k], lk_r.at[z], rows=row_id(to_z, x))

    def lk_arrival(shard):
        return remote(look.at[shard], L.at[shard], lk_s.at[0], lk_r.at[shard], rows=north)

    def x_copy(i, item):
        n = item[2]
        slot = n % SLOTS
        src, dst, to = [
            (stage.at[slot, 0], landing.at[n, 2], right),
            (stage.at[slot, 2], landing.at[n, 0], left),
            (stage.at[slot, 1, pl.ds(0, 64)], fwd_p.at[n], right),
            (stage.at[slot, 1, pl.ds(64, 64)], fwd_m.at[n], left),
            (fwd_p.at[n], landing.at[n, 1, pl.ds(0, 64)], right),
            (fwd_m.at[n], landing.at[n, 1, pl.ds(64, 64)], left),
        ][i]
        return remote(src, dst, x_s.at[n * 6 + i], x_r.at[n * 6 + i], rows=to)

    def columns(shard, place):
        for r in range(NX):
            line = jnp.broadcast_to(L[shard, pl.ds(lax.rem(x + r, NX), 1), :], (128, 128))
            LC[place, r] = jnp.transpose(line)

    def to_rows(value, h, first):
        for u in range(2):
            for j in range(4):
                flat[pl.ds((first + u * 8) * 8 + h * 4 + j, 8, stride=8), :] = value[
                    u * 8:(u + 1) * 8, j * 128:(j + 1) * 128
                ]

    def picked(h, shard, place, r):
        col = LC[place, r]
        lane = lax.broadcasted_iota(jnp.int32, (CAP, 128), 1)
        hot = jnp.concatenate(
            [jnp.where(col == lane + 128 * t, 1.0, 0.0) for t in range(NODES // 128)], axis=1
        ).astype(jnp.bfloat16)
        return jnp.dot(hot, T[h, shard], preferred_element_type=jnp.float32)

    def launch(item, place):
        h, shard, n = item
        if n >= SLOTS:
            for i in range(4):
                x_copy(i, (h, shard, n - SLOTS)).wait_send()

        @pl.loop(0, NX - 1)
        def _(r):
            stage[n % SLOTS, r] = picked(h, shard, place, r + 1).astype(jnp.bfloat16)

        for i in (2, 3, 0, 1):
            x_copy(i, item).start()
        own = picked(h, shard, place, 0) * 0.5
        for r in range(CAP // 16):
            to_rows(own[r * 16:(r + 1) * 16], h, (shard * NX + x) * CAP + r * 16)

    def forward(item):
        x_copy(2, item).wait_recv()
        x_copy(4, item).start()
        x_copy(3, item).wait_recv()
        x_copy(5, item).start()

    def unpack(item):
        h, shard, n = item
        for i in (0, 1, 4, 5):
            x_copy(i, item).wait_recv()

        for i in range(3):
            first = (shard * NX + lax.rem(x + i + 1, NX)) * CAP

            @pl.loop(0, CAP // 16)
            def _(r):
                value = landing[n, i, pl.ds(pl.multiple_of(r * 16, 16), 16), :]
                to_rows(value.astype(jnp.float32) * 0.5, h, first + r * 16)

    def grid_side(part):
        @pl.loop(part * 3, part * 3 + 3)
        def _(i):
            rows = pl.ds(pl.multiple_of(i * 128, 128), 128)
            for j in range(4):
                value = 0.5 * jnp.dot(
                    embed[rows, :], wdst[:, j * 256:(j + 1) * 256], preferred_element_type=jnp.float32
                )
                for r in range(16):
                    for t in range(2):
                        gs[pl.ds((i * 128 + r * 8) * 8 + j * 2 + t, 8, stride=8), :] = value[
                            r * 8:(r + 1) * 8, t * 128:(t + 1) * 128
                        ]

    L[z] = look[z]
    columns(z, 0)
    items = []
    for h in range(2):
        project(h)
        if h == 0:
            pl.semaphore_wait(barrier, len(peers))
        z_copy(0, 1, h).start()
        z_copy(1, 1, h).start()
        if h == 0:
            for k in range(1, NZ):
                lk_copy(k).start()
        items.append((h, z, h))
        launch(items[-1], 0)

    loads[0].wait()
    loads[1].wait()
    grid_side(0)
    grid_side(1)
    pending, landed = list(items), []
    for d in range(1, 5):
        below, above = lax.rem(z + NZ - d, NZ), lax.rem(z + d, NZ)
        for h in range(2):
            for direction in range(2):
                if d < 4 or direction == h:
                    z_copy(direction, d, h, arriving=True).wait_recv()
                    if d < 3 or (d == 3 and direction == h):
                        z_copy(direction, d + 1, h).start()
            shards = (below, above) if d < 4 else (below,)
            if h == 0:
                for i, shard in enumerate(shards):
                    lk_arrival(shard).wait_recv()
                    columns(shard, 1 + i)
            for item in pending:
                forward(item)
            ready, landed, pending = landed, pending, []
            for i, shard in enumerate(shards):
                items.append((h, shard, len(items)))
                pending.append(items[-1])
                launch(items[-1], 1 + i)
            for item in ready:
                unpack(item)
        if d == 1:
            grid_side(2)
            grid_side(3)
    for item in pending:
        forward(item)
    for item in landed + pending:
        unpack(item)

    for load in loads[2:]:
        load.wait()

    def m_copy(i, b, arriving=False):
        whose, to = [
            (m, up), (m, down), (m, partner),
            (down, up) if b % 2 == 0 else (up, down),
            (down, partner), (up, partner), (far, partner),
        ][i]
        if arriving:
            whose = [down, up, partner, far, down + other, up + other, far + other][i]
        return remote(X.at[whose, b], X.at[whose, b], m_s.at[b * 7 + i], m_r.at[b * 7 + i], member=to)

    def pass_on(b):
        first, second = (0, 1) if b % 2 == 0 else (1, 0)
        m_copy(first, b, True).wait_recv()
        m_copy(3, b).start()
        m_copy(4 + first, b).start()
        m_copy(second, b, True).wait_recv()
        m_copy(4 + second, b).start()

    def pass_far(b):
        m_copy(3, b, True).wait_recv()
        m_copy(6, b).start()

    gain_row = gain[...]
    for b in range(NB):
        @pl.loop(0, PB // 32)
        def _(q):
            for u in range(32):
                p = b * PB + q * 32 + u
                g = gs[pl.ds(pl.multiple_of(p * 8, 8), 8), :]
                total = jnp.zeros((8, 128), jnp.float32)
                for k in range(K):
                    half = F[edge[k, p]] + g
                    total = total + (half + half * jnp.tanh(half))
                S[pl.ds(q * 256 + (u // 8) * 64 + u % 8, 8, stride=8), :] = total

        cube = S[...].reshape(PB // 8, 8, 8, 128)
        summed = jnp.concatenate([cube[:, j].reshape(PB, 128) for j in range(8)], axis=1)
        scale = lax.rsqrt(jnp.mean(summed * summed, axis=-1, keepdims=True) + EPSILON)
        normed = (summed * scale * gain_row).astype(jnp.bfloat16)
        half = 0.5 * jnp.dot(normed, w_node[...], preferred_element_type=jnp.float32)
        hidden = (half + half * jnp.tanh(half)).astype(jnp.bfloat16)
        fields = lax.dot_general(
            w_out[...], hidden, (((1,), (1,)), ((), ())), preferred_element_type=jnp.float32
        )
        point = lax.broadcasted_iota(jnp.int32, (C, PB), 1) + b * PB
        fields = jnp.where(point < rp[0], fields, 0.0).astype(jnp.bfloat16)
        X[m, b, 0:C, :] = fields
        X[m, b, C:CP, :] = jnp.zeros((CP - C, PB), jnp.bfloat16)
        fields_out[:, b * PB:(b + 1) * PB] = fields
        for i in range(3):
            m_copy(i, b).start()
        if b >= 1:
            pass_on(b - 1)
        if b >= 2:
            pass_far(b - 2)

    def slope(v):
        return v * lax.rsqrt(v * v + SOFT_SCALE * SOFT_SCALE)

    wide = jnp.broadcast_to(weight[...], (C, 128))

    def score(b):
        for i in (2, 4, 5, 6):
            m_copy(i, b, True).wait_recv()

        @pl.loop(0, PB // 128)
        def _(t):
            lanes = pl.ds(pl.multiple_of(t * 128, 128), 128)
            whole = pl.ds(pl.multiple_of(b * PB + t * 128, 128), 128)
            here = X[m, b, 0:C, lanes].astype(jnp.float32)
            pair = jnp.zeros((C, 128), jnp.float32)
            for j in range(MEMBERS):
                pair = pair + slope(here - X[j, b, 0:C, lanes].astype(jnp.float32))
            total = slope(here - targets[:, whole]) - pair * (1.0 / (MEMBERS - 1))
            point = lax.broadcasted_iota(jnp.int32, (C, 128), 1) + b * PB + t * 128
            score_out[:, whole] = jnp.where(point < rp[0], wide * total, 0.0)

    score(0)
    pass_on(NB - 1)
    score(1)
    pass_far(NB - 2)
    score(2)
    pass_far(NB - 1)
    for b in range(3, NB):
        score(b)

    for item in items:
        for i in range(6):
            if i >= 4 or item[2] >= len(items) - SLOTS:
                x_copy(i, item).wait_send()
    for d in range(1, 5):
        for h in range(2):
            for direction in range(2):
                if d < 4 or h == direction:
                    z_copy(direction, d, h).wait_send()
    for k in range(1, NZ):
        lk_copy(k).wait_send()
    for b in range(NB):
        for i in range(7):
            m_copy(i, b).wait_send()


def decoder_call(edge, rp, latent, w_src, look, gain, weight, embed, w_dst, w_node, w_out, targets):
    n_items = 2 * NZ
    vm = pl.BlockSpec(memory_space=pltpu.VMEM)
    sm = pl.BlockSpec(memory_space=pltpu.SMEM)
    hbm = pl.BlockSpec(memory_space=pl.ANY)
    dma = pltpu.SemaphoreType.DMA
    half, full = jnp.bfloat16, jnp.float32
    return pl.pallas_call(
        decoder_kernel,
        out_shape=(
            jax.ShapeDtypeStruct((C, G), half),
            jax.ShapeDtypeStruct((C, G), full),
        ),
        in_specs=[sm, sm, vm, vm, vm, vm, vm, hbm, hbm, hbm, hbm, hbm],
        out_specs=(vm, vm),
        scratch_shapes=[
            pltpu.VMEM((2, NZ, NODES, W), half),
            pltpu.VMEM((SLOTS, NX - 1, CAP, W), half),
            pltpu.VMEM((n_items, NX - 1, CAP, W), half),
            pltpu.VMEM((n_items, 64, W), half),
            pltpu.VMEM((n_items, 64, W), half),
            pltpu.VMEM((NZ, NX, CAP), jnp.int32),
            pltpu.VMEM((3, NX, CAP, 128), jnp.int32),
            pltpu.VMEM((ROWS * CAP, 8, 128), full),
            pltpu.VMEM((G * 8, 128), full),
            pltpu.VMEM((PB * 8, 128), full),
            pltpu.VMEM((MEMBERS, NB, CP, PB), half),
            pltpu.VMEM((G, D), half),
            pltpu.VMEM((D, D), half),
            pltpu.VMEM((D, D), half),
            pltpu.VMEM((C, D), half),
            pltpu.VMEM((C, G), full),
            dma((NZ,)), dma((NZ,)),
            dma((16,)), dma((16,)),
            dma((n_items * 6,)), dma((n_items * 6,)),
            dma((NB * 7,)), dma((NB * 7,)),
            dma((5,)),
        ],
        compiler_params=pltpu.CompilerParams(
            collective_id=0, has_side_effects=True, vmem_limit_bytes=VMEM_LIMIT
        ),
        cost_estimate=pl.CostEstimate(flops=14 * 10**9, bytes_accessed=20 * MIB, transcendentals=0),
        name="decoder",
    )(edge, rp, latent, w_src, look, gain, weight, embed, w_dst, w_node, w_out, targets)


def local(
    processed_latent_nodes, grid_embed, dispatch_node_lookup, send_count, edge_slot, row_points,
    w_src, w_dst, gain_node, w_node, w_out, targets, channel_weight,
):
    del send_count
    fields, score = decoder_call(
        edge_slot, row_points, processed_latent_nodes[0], w_src,
        dispatch_node_lookup.reshape(NZ, NX, CAP), gain_node[None, :], channel_weight[:, None],
        grid_embed, w_dst, w_node, w_out, targets,
    )
    return fields[None], score[None]


def solution(mesh):
    placed = (
        P("member", "rows", None),
        P("rows", None),
        P("rows", None),
        P("rows"),
        P(None, "rows"),
        P("rows"),
        P(),
        P(),
        P(),
        P(),
        P(),
        P(None, "rows"),
        P(),
    )
    return jax.shard_map(
        local,
        mesh=mesh,
        in_specs=placed,
        out_specs=(P("member", None, "rows"), P("member", None, "rows")),
        check_vma=False,
    )
```

time: 372 us -> 147 us (0.40)
  the two profiles are of different devices: /device:TPU:102 before, /device:TPU:1 now
where the time goes in v2:
time: 147 us; the launch traced here: 146 us
  Pallas kernels  140 us (95%)
  local copies, waits for them, and re-layouts  5.63 us (4%)
    pallas_call x1, Pallas kernels, decoder_call(): pl.pallas_call(decoder_kernel, out_shape=(jax.ShapeDtypeStruct((C, G), ha...  140 us
    unnamed x2, local copies, waits for them, and re-layouts  4.25 us

profile of v2, /device:TPU:1, one launch (start us, length us, event | category | flops | bytes accessed | tf_op | source)
XLA Modules:
  0.0 146.5 jit_solution(11678051276972585534)
XLA Ops:
  1.3 1.4 copy.14.weight
  2.7 139.6 %decoder.1 = (bf16[100,1536]{1,0:T(8,128)(2,1)}, f32[100,1536]{1,0:T(8,128)}) custom-call(s32[3,1536]{1,0:T(4,128)} %edge.1, s32[1]{0:T(128)S(6)} %copy.17.rp, bf16[512,1024]{1,0:T(8,128)(2,1)} %bitcast.9, bf16[1024,1024]{1,0:T(8,128)(2,1)} %w_src.1, s32[8,4,128]{2,1,0:T(4,128)} %bitcast.10, f32[1,1024]{1,0:T(1,128)} %bitcast.11, f32[100,1]{1,0:T(8,128)} %copy.14.weight, ...), custom_call_target="tpu_custom_call" | custom-call | flops 14000000000 | bytes 20971520 | tf_op jit(solution)/shard_map/decoder/pallas_call | solution.py:353
  142.2 2.5 %copy.15 = f32[1,100,1536]{2,0,1:T(1,128)} copy(f32[1,100,1536]{2,1,0:T(8,128)} %bitcast.6) | data formatting | bytes 1228800
  144.8 1.7 %copy.18 = bf16[1,100,1536]{2,1,0:T(8,128)(2,1)} copy(bf16[1,100,1536]{2,1,0:T(8,128)(2,1)} %bitcast.7) | data formatting | bytes 614400

commit v3 on v2

v3 whole, which is shorter than its diff:
```python
import functools

import jax
import jax.numpy as jnp
from jax import lax
from jax.experimental import pallas as pl
from jax.experimental.pallas import tpu as pltpu
from jax.sharding import PartitionSpec as P

SOFT_SCALE = 0.5
EPSILON = 1e-05
MESH = pl.DeviceIdType.MESH

NZ, NX, NY = 8, 4, 4
ROWS = NZ * NX
MEMBERS = 8
CAP = 128
NODES = 512
D = 1024
W = 256
Q = D // W
G = 1536
C = 100
CP = 112
K = 3
PB = 256
NB = G // PB
SLOTS = 16
MIB = 1 << 20
VMEM_LIMIT = 60 * MIB


def row_id(z, x):
    return lax.rem(z, NZ) * NX + lax.rem(x, NX)


def decoder_kernel(
    edge, rp, latent, w_src, look, gain, weight,
    embed_hbm, wdst_hbm, wnode_hbm, wout_hbm, targets_hbm,
    fields_out, score_out,
    T, stage, landing, L, hot, F, gs, S, X,
    embed, square, w_out, targets,
    lk_s, lk_r, z_s, z_r, x_s, x_r, m_s, m_r, pre,
):
    me = lax.axis_index("rows")
    z = me // NX
    x = lax.rem(me, NX)
    m = lax.axis_index("member")
    y = m // 2
    c = lax.rem(m, 2)
    north, south = row_id(z + 1, x), row_id(z + NZ - 1, x)

    flat = F.reshape(ROWS * CAP * 8, 128)

    def chip(k):
        return lax.rem(y + k, NY) * 2

    up, down, far, partner = chip(1) + c, chip(3) + c, chip(2) + c, chip(0) + 1 - c
    other = 1 - 2 * c

    barrier = pltpu.get_barrier_semaphore()
    peers = [{"rows": row_id(z + k, x)} for k in range(1, NZ)]
    peers += [{"rows": row_id(z, x + k)} for k in range(1, NX)]
    peers += [{"member": up}, {"member": down}, {"member": partner}]
    for peer in peers:
        pl.semaphore_signal(barrier, inc=1, device_id=peer, device_id_type=MESH)

    loads = [
        pltpu.make_async_copy(a, b, pre.at[i])
        for i, (a, b) in enumerate([
            (embed_hbm, embed), (wdst_hbm, square), (wout_hbm, w_out), (targets_hbm, targets),
        ])
    ]
    for load in loads:
        load.start()
    load_node = pltpu.make_async_copy(wnode_hbm, square, pre.at[4])

    def remote(src, dst, ss, rs, **to):
        return pltpu.make_async_remote_copy(
            src_ref=src, dst_ref=dst, send_sem=ss, recv_sem=rs,
            device_id=to, device_id_type=MESH,
        )

    def project(q):
        T[q, z] = jnp.dot(
            latent[...], w_src[:, q * W:(q + 1) * W], preferred_element_type=jnp.float32
        ).astype(jnp.bfloat16)

    def z_copy(direction, d, q, arriving=False):
        back = d if arriving else d - 1
        shard = lax.rem(z + NZ - back, NZ) if direction == 0 else lax.rem(z + back, NZ)
        i = (direction * 4 + d - 1) * Q + q
        return remote(
            T.at[q, shard], T.at[q, shard], z_s.at[i], z_r.at[i],
            rows=north if direction == 0 else south,
        )

    def goes(direction, d, q):
        return d < 4 or q % 2 == direction

    def lk_copy(k):
        to_z = lax.rem(z + k, NZ)
        return remote(look.at[to_z], L.at[z], lk_s.at[k], lk_r.at[z], rows=row_id(to_z, x))

    def lk_arrival(shard):
        return remote(look.at[shard], L.at[shard], lk_s.at[0], lk_r.at[shard], rows=north)

    def x_copy(i, item):
        n = item[2]
        to = row_id(z, x + 1 + i)
        return remote(
            stage.at[n % SLOTS, i], landing.at[n, 2 - i], x_s.at[n * 3 + i], x_r.at[n * 3 + i], rows=to
        )

    def choose(shard, place):
        for r in range(NX):
            line = jnp.broadcast_to(L[shard, pl.ds(lax.rem(x + r, NX), 1), :], (CAP, 128))
            col = jnp.transpose(line)
            lane = lax.broadcasted_iota(jnp.int32, (CAP, 128), 1)
            for t in range(NODES // 128):
                hot[place, r * CAP:(r + 1) * CAP, t * 128:(t + 1) * 128] = jnp.where(
                    col == lane + 128 * t, 1.0, 0.0
                ).astype(jnp.bfloat16)

    def to_rows(value, q, first):
        for u in range(2):
            for j in range(W // 128):
                flat[pl.ds((first + u * 8) * 8 + q * (W // 128) + j, 8, stride=8), :] = value[
                    u * 8:(u + 1) * 8, j * 128:(j + 1) * 128
                ]

    def launch(item, place):
        q, shard, n = item
        if n >= SLOTS:
            for i in range(NX - 1):
                x_copy(i, (q, shard, n - SLOTS)).wait_send()
        picked = jnp.dot(hot[place], T[q, shard], preferred_element_type=jnp.float32)
        for i in range(NX - 1):
            stage[n % SLOTS, i] = picked[(i + 1) * CAP:(i + 2) * CAP].astype(jnp.bfloat16)
        for i in (1, 0, 2):
            x_copy(i, item).start()
        for r in range(CAP // 16):
            to_rows(picked[r * 16:(r + 1) * 16] * 0.5, q, (shard * NX + x) * CAP + r * 16)

    def unpack(item):
        q, shard, n = item
        for i in range(NX - 1):
            x_copy(i, item).wait_recv()

        for i in range(NX - 1):
            first = (shard * NX + lax.rem(x + i + 1, NX)) * CAP

            @pl.loop(0, CAP // 32)
            def _(r):
                value = landing[n, i, pl.ds(pl.multiple_of(r * 32, 32), 32), :].astype(jnp.float32) * 0.5
                for v in range(2):
                    to_rows(value[v * 16:(v + 1) * 16], q, first + r * 32 + v * 16)

    def grid_side(i):
        for j in range(D // 256):
            value = 0.5 * jnp.dot(
                embed[i * 128:(i + 1) * 128, :], square[:, j * 256:(j + 1) * 256],
                preferred_element_type=jnp.float32,
            )
            for r in range(16):
                for t in range(2):
                    gs[pl.ds((i * 128 + r * 8) * 8 + j * 2 + t, 8, stride=8), :] = value[
                        r * 8:(r + 1) * 8, t * 128:(t + 1) * 128
                    ]

    L[z] = look[z]
    choose(z, 0)
    items = []
    for q in range(Q):
        project(q)
        if q == 0:
            pl.semaphore_wait(barrier, len(peers))
        z_copy(0, 1, q).start()
        z_copy(1, 1, q).start()
        if q == 0:
            for k in range(1, NZ):
                lk_copy(k).start()
        items.append((q, z, q))
        launch(items[-1], 0)

    loads[0].wait()
    loads[1].wait()
    landed = [items[0:2], items[2:4]]
    step = 0
    for d in range(1, 5):
        below, above = lax.rem(z + NZ - d, NZ), lax.rem(z + d, NZ)
        shards = (below, above) if d < 4 else (below,)
        for q in range(Q):
            for direction in range(2):
                if goes(direction, d, q):
                    z_copy(direction, d, q, arriving=True).wait_recv()
                    if d < 4 and goes(direction, d + 1, q):
                        z_copy(direction, d + 1, q).start()
            if q == 0:
                for i, shard in enumerate(shards):
                    lk_arrival(shard).wait_recv()
                    choose(shard, 1 + i)
            new = []
            for i, shard in enumerate(shards):
                items.append((q, shard, len(items)))
                new.append(items[-1])
                launch(items[-1], 1 + i)
            landed.append(new)
            if step < G // 128:
                grid_side(step)
            if step == G // 128:
                load_node.start()
            if len(landed) > 3:
                for item in landed.pop(0):
                    unpack(item)
            step += 1
    for group in landed:
        for item in group:
            unpack(item)

    loads[2].wait()
    loads[3].wait()
    load_node.wait()

    def m_copy(i, b, arriving=False):
        whose, to = [
            (m, up), (m, down), (m, partner),
            (down, up) if b % 2 == 0 else (up, down),
            (down, partner), (up, partner), (far, partner),
        ][i]
        if arriving:
            whose = [down, up, partner, far, down + other, up + other, far + other][i]
        return remote(X.at[whose, b], X.at[whose, b], m_s.at[b * 7 + i], m_r.at[b * 7 + i], member=to)

    def pass_on(b):
        first, second = (0, 1) if b % 2 == 0 else (1, 0)
        m_copy(first, b, True).wait_recv()
        m_copy(3, b).start()
        m_copy(4 + first, b).start()
        m_copy(second, b, True).wait_recv()
        m_copy(4 + second, b).start()

    def pass_far(b):
        m_copy(3, b, True).wait_recv()
        m_copy(6, b).start()

    gain_row = gain[...]
    for b in range(NB):
        @pl.loop(0, PB // 32)
        def _(q):
            for u in range(32):
                p = b * PB + q * 32 + u
                g = gs[pl.ds(pl.multiple_of(p * 8, 8), 8), :]
                total = jnp.zeros((8, 128), jnp.float32)
                for k in range(K):
                    half = F[edge[k, p]] + g
                    total = total + (half + half * jnp.tanh(half))
                S[pl.ds(q * 256 + (u // 8) * 64 + u % 8, 8, stride=8), :] = total

        cube = S[...].reshape(PB // 8, 8, 8, 128)
        summed = jnp.concatenate([cube[:, j].reshape(PB, 128) for j in range(8)], axis=1)
        scale = lax.rsqrt(jnp.mean(summed * summed, axis=-1, keepdims=True) + EPSILON)
        normed = (summed * scale * gain_row).astype(jnp.bfloat16)
        half = 0.5 * jnp.dot(normed, square[...], preferred_element_type=jnp.float32)
        hidden = (half + half * jnp.tanh(half)).astype(jnp.bfloat16)
        fields = lax.dot_general(
            w_out[...], hidden, (((1,), (1,)), ((), ())), preferred_element_type=jnp.float32
        )
        point = lax.broadcasted_iota(jnp.int32, (C, PB), 1) + b * PB
        fields = jnp.where(point < rp[0], fields, 0.0).astype(jnp.bfloat16)
        X[m, b, 0:C, :] = fields
        X[m, b, C:CP, :] = jnp.zeros((CP - C, PB), jnp.bfloat16)
        fields_out[:, b * PB:(b + 1) * PB] = fields
        for i in range(3):
            m_copy(i, b).start()
        if b >= 2:
            pass_on(b - 2)
        if b >= 4:
            pass_far(b - 4)

    def slope(v):
        return v * lax.rsqrt(v * v + SOFT_SCALE * SOFT_SCALE)

    line = jnp.concatenate([weight[...], jnp.zeros((1, 128 - C), jnp.float32)], axis=1)
    wide = jnp.transpose(jnp.broadcast_to(line, (128, 128)))[0:C, :]

    def score(b):
        for i in (2, 4, 5, 6):
            m_copy(i, b, True).wait_recv()

        @pl.loop(0, PB // 128)
        def _(t):
            lanes = pl.ds(pl.multiple_of(t * 128, 128), 128)
            whole = pl.ds(pl.multiple_of(b * PB + t * 128, 128), 128)
            here = X[m, b, 0:C, lanes].astype(jnp.float32)
            pair = jnp.zeros((C, 128), jnp.float32)
            for j in range(MEMBERS):
                pair = pair + slope(here - X[j, b, 0:C, lanes].astype(jnp.float32))
            total = slope(here - targets[:, whole]) - pair * (1.0 / (MEMBERS - 1))
            point = lax.broadcasted_iota(jnp.int32, (C, 128), 1) + b * PB + t * 128
            score_out[:, whole] = jnp.where(point < rp[0], wide * total, 0.0)

    pass_far(NB - 4)
    pass_on(NB - 2)
    score(0)
    pass_far(NB - 3)
    score(1)
    pass_on(NB - 1)
    score(2)
    pass_far(NB - 2)
    score(3)
    pass_far(NB - 1)
    score(4)
    score(5)

    for item in items[-SLOTS:]:
        for i in range(NX - 1):
            x_copy(i, item).wait_send()
    for d in range(1, 5):
        for q in range(Q):
            for direction in range(2):
                if goes(direction, d, q):
                    z_copy(direction, d, q).wait_send()
    for k in range(1, NZ):
        lk_copy(k).wait_send()
    for b in range(NB):
        for i in range(7):
            m_copy(i, b).wait_send()


def decoder_call(edge, rp, latent, w_src, look, gain, weight, embed, w_dst, w_node, w_out, targets):
    n_items = Q * NZ
    vm = pl.BlockSpec(memory_space=pltpu.VMEM)
    sm = pl.BlockSpec(memory_space=pltpu.SMEM)
    hbm = pl.BlockSpec(memory_space=pl.ANY)
    dma = pltpu.SemaphoreType.DMA
    half, full = jnp.bfloat16, jnp.float32
    return pl.pallas_call(
        decoder_kernel,
        out_shape=(
            jax.ShapeDtypeStruct((C, G), half),
            jax.ShapeDtypeStruct((C, G), full),
        ),
        in_specs=[sm, sm, vm, vm, vm, vm, vm, hbm, hbm, hbm, hbm, hbm],
        out_specs=(vm, vm),
        scratch_shapes=[
            pltpu.VMEM((Q, NZ, NODES, W), half),
            pltpu.VMEM((SLOTS, NX - 1, CAP, W), half),
            pltpu.VMEM((n_items, NX - 1, CAP, W), half),
            pltpu.VMEM((NZ, NX, CAP), jnp.int32),
            pltpu.VMEM((3, NX * CAP, NODES), half),
            pltpu.VMEM((ROWS * CAP, 8, 128), full),
            pltpu.VMEM((G * 8, 128), full),
            pltpu.VMEM((PB * 8, 128), full),
            pltpu.VMEM((MEMBERS, NB, CP, PB), half),
            pltpu.VMEM((G, D), half),
            pltpu.VMEM((D, D), half),
            pltpu.VMEM((C, D), half),
            pltpu.VMEM((C, G), full),
            dma((NZ,)), dma((NZ,)),
            dma((8 * Q,)), dma((8 * Q,)),
            dma((n_items * 3,)), dma((n_items * 3,)),
            dma((NB * 7,)), dma((NB * 7,)),
            dma((5,)),
        ],
        compiler_params=pltpu.CompilerParams(
            collective_id=0, has_side_effects=True, vmem_limit_bytes=VMEM_LIMIT
        ),
        cost_estimate=pl.CostEstimate(flops=14 * 10**9, bytes_accessed=20 * MIB, transcendentals=0),
        name="decoder",
    )(edge, rp, latent, w_src, look, gain, weight, embed, w_dst, w_node, w_out, targets)


def local(
    processed_latent_nodes, grid_embed, dispatch_node_lookup, send_count, edge_slot, row_points,
    w_src, w_dst, gain_node, w_node, w_out, targets, channel_weight,
):
    del send_count
    fields, score = decoder_call(
        edge_slot, row_points, processed_latent_nodes[0], w_src,
        dispatch_node_lookup.reshape(NZ, NX, CAP), gain_node[None, :], channel_weight[None, :],
        grid_embed, w_dst, w_node, w_out, targets,
    )
    return fields[None], score[None]


def solution(mesh):
    placed = (
        P("member", "rows", None),
        P("rows", None),
        P("rows", None),
        P("rows"),
        P(None, "rows"),
        P("rows"),
        P(),
        P(),
        P(),
        P(),
        P(),
        P(None, "rows"),
        P(),
    )
    return jax.shard_map(
        local,
        mesh=mesh,
        in_specs=placed,
        out_specs=(P("member", None, "rows"), P("member", None, "rows")),
        check_vma=False,
    )
```

time: 147 us -> 139 us (0.946)
  Pallas kernels: 140 us -> 133 us
    pallas_call x1, Pallas kernels: 140 us -> 133 us  [decoder_call(): pl.pallas_call(decoder_kernel, out_shape=(jax.ShapeDtypeStruct((C, G), ha...]
where the time goes in v3:
time: 139 us
  Pallas kernels  133 us (96%)
  local copies, waits for them, and re-layouts  4.25 us (3%)
    pallas_call x1, Pallas kernels, decoder_call(): pl.pallas_call(decoder_kernel, out_shape=(jax.ShapeDtypeStruct((C, G), ha...  133 us
    unnamed x2, local copies, waits for them, and re-layouts  4.25 us

profile of v3, /device:TPU:1, one launch (start us, length us, event | category | flops | bytes accessed | tf_op | source)
XLA Modules:
  0.0 138.7 jit_solution(15382453290837873928)
XLA Ops:
  1.3 133.2 %decoder.1 = (bf16[100,1536]{1,0:T(8,128)(2,1)}, f32[100,1536]{1,0:T(8,128)}) custom-call(s32[3,1536]{1,0:T(4,128)} %edge.1, s32[1]{0:T(128)S(6)} %copy.16.rp, bf16[512,1024]{1,0:T(8,128)(2,1)} %bitcast.8, bf16[1024,1024]{1,0:T(8,128)(2,1)} %w_src.1, s32[8,4,128]{2,1,0:T(4,128)} %bitcast.9, f32[1,1024]{1,0:T(1,128)} %bitcast.10, f32[1,100]{1,0:T(1,128)} %bitcast.11, ...), custom_call_target="tpu_custom_call" | custom-call | flops 14000000000 | bytes 20971520 | tf_op jit(solution)/shard_map/decoder/pallas_call | solution.py:338
  134.5 2.5 %copy.14 = f32[1,100,1536]{2,0,1:T(1,128)} copy(f32[1,100,1536]{2,1,0:T(8,128)} %bitcast.6) | data formatting | bytes 1228800
  137.0 1.7 %copy.17 = bf16[1,100,1536]{2,1,0:T(8,128)(2,1)} copy(bf16[1,100,1536]{2,1,0:T(8,128)(2,1)} %bitcast.7) | data formatting | bytes 614400

commit v4 on v3

--- a/solution.py
+++ b/solution.py
@@ -24,10 +24,11 @@
 CP = 112
 K = 3
 PB = 256
-NB = G // PB
+BLOCKS = [(i * PB, PB) for i in range(5)] + [(5 * PB, 128), (5 * PB + 128, 128)]
+NB = len(BLOCKS)
 SLOTS = 16
 MIB = 1 << 20
-VMEM_LIMIT = 60 * MIB
+VMEM_LIMIT = 56 * MIB
 
 
 def row_id(z, x):
@@ -35,12 +36,12 @@
 
 
 def decoder_kernel(
-    edge, rp, latent, w_src, look, gain, weight,
-    embed_hbm, wdst_hbm, wnode_hbm, wout_hbm, targets_hbm,
+    edge, look, gain, weight,
+    rp_hbm, latent_hbm, wsrc_hbm, embed_hbm, wdst_hbm, wnode_hbm, wout_hbm, targets_hbm,
     fields_out, score_out,
     T, stage, landing, L, hot, F, gs, S, X,
-    embed, square, w_out, targets,
-    lk_s, lk_r, z_s, z_r, x_s, x_r, m_s, m_r, pre,
+    fields_all, rp, latent, w_src, embed, square, w_out, targets,
+    lk_s, lk_r, z_s, z_r, x_s, x_r, m_s, m_r, pre, first,
 ):
     me = lax.axis_index("rows")
     z = me // NX
@@ -61,19 +62,23 @@
     barrier = pltpu.get_barrier_semaphore()
     peers = [{"rows": row_id(z + k, x)} for k in range(1, NZ)]
     peers += [{"rows": row_id(z, x + k)} for k in range(1, NX)]
-    peers += [{"member": up}, {"member": down}, {"member": partner}]
+    peers += [{"member": lax.rem(m + k, MEMBERS)} for k in range(1, MEMBERS)]
     for peer in peers:
         pl.semaphore_signal(barrier, inc=1, device_id=peer, device_id_type=MESH)
 
+    head = [pltpu.make_async_copy(latent_hbm, latent, first.at[Q])]
+    for q in range(Q):
+        cols = pl.ds(q * W, W)
+        head.append(pltpu.make_async_copy(wsrc_hbm.at[:, cols], w_src.at[q], first.at[q]))
     loads = [
         pltpu.make_async_copy(a, b, pre.at[i])
         for i, (a, b) in enumerate([
-            (embed_hbm, embed), (wdst_hbm, square), (wout_hbm, w_out), (targets_hbm, targets),
+            (embed_hbm, embed), (wdst_hbm, square), (wout_hbm, w_out), (targets_hbm, targets), (rp_hbm, rp),
         ])
     ]
-    for load in loads:
+    for load in head + loads:
         load.start()
-    load_node = pltpu.make_async_copy(wnode_hbm, square, pre.at[4])
+    load_node = pltpu.make_async_copy(wnode_hbm, square, pre.at[5])
 
     def remote(src, dst, ss, rs, **to):
         return pltpu.make_async_remote_copy(
@@ -83,7 +88,7 @@
 
     def project(q):
         T[q, z] = jnp.dot(
-            latent[...], w_src[:, q * W:(q + 1) * W], preferred_element_type=jnp.float32
+            latent[...], w_src[q], preferred_element_type=jnp.float32
         ).astype(jnp.bfloat16)
 
     def z_copy(direction, d, q, arriving=False):
@@ -171,7 +176,9 @@
     L[z] = look[z]
     choose(z, 0)
     items = []
+    head[0].wait()
     for q in range(Q):
+        head[1 + q].wait()
         project(q)
         if q == 0:
             pl.semaphore_wait(barrier, len(peers))
@@ -220,22 +227,29 @@
 
     loads[2].wait()
     loads[3].wait()
+    loads[4].wait()
     load_node.wait()
 
     def m_copy(i, b, arriving=False):
-        whose, to = [
-            (m, up), (m, down), (m, partner),
-            (down, up) if b % 2 == 0 else (up, down),
-            (down, partner), (up, partner), (far, partner),
-        ][i]
+        if b == NB - 1:
+            whose = m
+            to = [up, down, partner, far, up + other, down + other, far + other][i]
+        else:
+            whose, to = [
+                (m, up), (m, down), (m, partner),
+                (m, far) if b >= NB - 3 else (down, up) if b % 2 == 0 else (up, down),
+                (down, partner), (up, partner), (far, partner),
+            ][i]
         if arriving:
             whose = [down, up, partner, far, down + other, up + other, far + other][i]
-        return remote(X.at[whose, b], X.at[whose, b], m_s.at[b * 7 + i], m_r.at[b * 7 + i], member=to)
+        spot = X.at[whose, :, pl.ds(*BLOCKS[b])]
+        return remote(spot, spot, m_s.at[b * 7 + i], m_r.at[b * 7 + i], member=to)
 
     def pass_on(b):
         first, second = (0, 1) if b % 2 == 0 else (1, 0)
         m_copy(first, b, True).wait_recv()
-        m_copy(3, b).start()
+        if b < NB - 3:
+            m_copy(3, b).start()
         m_copy(4 + first, b).start()
         m_copy(second, b, True).wait_recv()
         m_copy(4 + second, b).start()
@@ -245,11 +259,17 @@
         m_copy(6, b).start()
 
     gain_row = gain[...]
+
+    limit = rp[0]
+    save_fields = pltpu.make_async_copy(fields_all, fields_out, pre.at[6])
+
     for b in range(NB):
-        @pl.loop(0, PB // 32)
+        start, size = BLOCKS[b]
+
+        @pl.loop(0, size // 32)
         def _(q):
             for u in range(32):
-                p = b * PB + q * 32 + u
+                p = start + q * 32 + u
                 g = gs[pl.ds(pl.multiple_of(p * 8, 8), 8), :]
                 total = jnp.zeros((8, 128), jnp.float32)
                 for k in range(K):
@@ -257,8 +277,8 @@
                     total = total + (half + half * jnp.tanh(half))
                 S[pl.ds(q * 256 + (u // 8) * 64 + u % 8, 8, stride=8), :] = total
 
-        cube = S[...].reshape(PB // 8, 8, 8, 128)
-        summed = jnp.concatenate([cube[:, j].reshape(PB, 128) for j in range(8)], axis=1)
+        cube = S[0:size * 8, :].reshape(size // 8, 8, 8, 128)
+        summed = jnp.concatenate([cube[:, j].reshape(size, 128) for j in range(8)], axis=1)
         scale = lax.rsqrt(jnp.mean(summed * summed, axis=-1, keepdims=True) + EPSILON)
         normed = (summed * scale * gain_row).astype(jnp.bfloat16)
         half = 0.5 * jnp.dot(normed, square[...], preferred_element_type=jnp.float32)
@@ -266,13 +286,15 @@
         fields = lax.dot_general(
             w_out[...], hidden, (((1,), (1,)), ((), ())), preferred_element_type=jnp.float32
         )
-        point = lax.broadcasted_iota(jnp.int32, (C, PB), 1) + b * PB
-        fields = jnp.where(point < rp[0], fields, 0.0).astype(jnp.bfloat16)
-        X[m, b, 0:C, :] = fields
-        X[m, b, C:CP, :] = jnp.zeros((CP - C, PB), jnp.bfloat16)
-        fields_out[:, b * PB:(b + 1) * PB] = fields
-        for i in range(3):
+        point = lax.broadcasted_iota(jnp.int32, (C, size), 1) + start
+        fields = jnp.where(point < limit, fields, 0.0).astype(jnp.bfloat16)
+        X[m, 0:C, start:start + size] = fields
+        X[m, C:CP, start:start + size] = jnp.zeros((CP - C, size), jnp.bfloat16)
+        for i in range(7 if b == NB - 1 else 4 if b >= NB - 3 else 3):
             m_copy(i, b).start()
+        fields_all[:, start:start + size] = fields
+        if b == NB - 1:
+            save_fields.start()
         if b >= 2:
             pass_on(b - 2)
         if b >= 4:
@@ -285,33 +307,30 @@
     wide = jnp.transpose(jnp.broadcast_to(line, (128, 128)))[0:C, :]
 
     def score(b):
-        for i in (2, 4, 5, 6):
+        start, size = BLOCKS[b]
+        for i in (range(7) if b == NB - 1 else (2, 4, 5, 6)):
             m_copy(i, b, True).wait_recv()
 
-        @pl.loop(0, PB // 128)
+        @pl.loop(0, size // 128)
         def _(t):
-            lanes = pl.ds(pl.multiple_of(t * 128, 128), 128)
-            whole = pl.ds(pl.multiple_of(b * PB + t * 128, 128), 128)
-            here = X[m, b, 0:C, lanes].astype(jnp.float32)
+            tile = start // 128 + t
+            lanes = pl.ds(pl.multiple_of(tile * 128, 128), 128)
+            here = X[m, 0:C, lanes].astype(jnp.float32)
             pair = jnp.zeros((C, 128), jnp.float32)
-            for j in range(MEMBERS):
-                pair = pair + slope(here - X[j, b, 0:C, lanes].astype(jnp.float32))
-            total = slope(here - targets[:, whole]) - pair * (1.0 / (MEMBERS - 1))
-            point = lax.broadcasted_iota(jnp.int32, (C, 128), 1) + b * PB + t * 128
-            score_out[:, whole] = jnp.where(point < rp[0], wide * total, 0.0)
+            for k in range(1, MEMBERS):
+                pair = pair + slope(here - X[lax.rem(m + k, MEMBERS), 0:C, lanes].astype(jnp.float32))
+            total = slope(here - targets[:, lanes]) - pair * (1.0 / (MEMBERS - 1))
+            point = lax.broadcasted_iota(jnp.int32, (C, 128), 1) + tile * 128
+            score_out[pl.ds(tile, C, stride=G // 128), :] = jnp.where(point < limit, wide * total, 0.0)
 
     pass_far(NB - 4)
-    pass_on(NB - 2)
     score(0)
     pass_far(NB - 3)
+    pass_on(NB - 2)
     score(1)
-    pass_on(NB - 1)
-    score(2)
     pass_far(NB - 2)
-    score(3)
-    pass_far(NB - 1)
-    score(4)
-    score(5)
+    for b in range(2, NB):
+        score(b)
 
     for item in items[-SLOTS:]:
         for i in range(NX - 1):
@@ -326,23 +345,24 @@
     for b in range(NB):
         for i in range(7):
             m_copy(i, b).wait_send()
-
-
-def decoder_call(edge, rp, latent, w_src, look, gain, weight, embed, w_dst, w_node, w_out, targets):
+    save_fields.wait()
+
+
+def decoder_call(edge, look, gain, weight, *arrays):
     n_items = Q * NZ
     vm = pl.BlockSpec(memory_space=pltpu.VMEM)
     sm = pl.BlockSpec(memory_space=pltpu.SMEM)
-    hbm = pl.BlockSpec(memory_space=pl.ANY)
+    hbm = pl.BlockSpec(memory_space=pltpu.HBM)
     dma = pltpu.SemaphoreType.DMA
     half, full = jnp.bfloat16, jnp.float32
     return pl.pallas_call(
         decoder_kernel,
         out_shape=(
             jax.ShapeDtypeStruct((C, G), half),
-            jax.ShapeDtypeStruct((C, G), full),
+            jax.ShapeDtypeStruct((C * (G // 128), 128), full),
         ),
-        in_specs=[sm, sm, vm, vm, vm, vm, vm, hbm, hbm, hbm, hbm, hbm],
-        out_specs=(vm, vm),
+        in_specs=[sm, vm, vm, vm] + [hbm] * len(arrays),
+        out_specs=(hbm, vm),
         scratch_shapes=[
             pltpu.VMEM((Q, NZ, NODES, W), half),
             pltpu.VMEM((SLOTS, NX - 1, CAP, W), half),
@@ -352,7 +372,11 @@
             pltpu.VMEM((ROWS * CAP, 8, 128), full),
             pltpu.VMEM((G * 8, 128), full),
             pltpu.VMEM((PB * 8, 128), full),
-            pltpu.VMEM((MEMBERS, NB, CP, PB), half),
+            pltpu.VMEM((MEMBERS, CP, G), half),
+            pltpu.VMEM((C, G), half),
+            pltpu.SMEM((1,), jnp.int32),
+            pltpu.VMEM((NODES, D), half),
+            pltpu.VMEM((Q, D, W), half),
             pltpu.VMEM((G, D), half),
             pltpu.VMEM((D, D), half),
             pltpu.VMEM((C, D), half),
@@ -361,14 +385,38 @@
             dma((8 * Q,)), dma((8 * Q,)),
             dma((n_items * 3,)), dma((n_items * 3,)),
             dma((NB * 7,)), dma((NB * 7,)),
-            dma((5,)),
+            dma((7,)), dma((Q + 1,)),
         ],
         compiler_params=pltpu.CompilerParams(
             collective_id=0, has_side_effects=True, vmem_limit_bytes=VMEM_LIMIT
         ),
         cost_estimate=pl.CostEstimate(flops=14 * 10**9, bytes_accessed=20 * MIB, transcendentals=0),
         name="decoder",
-    )(edge, rp, latent, w_src, look, gain, weight, embed, w_dst, w_node, w_out, targets)
+    )(edge, look, gain, weight, *arrays)
+
+
+def place_kernel(a, b, a_out, b_out, sems):
+    copies = [
+        pltpu.make_async_copy(a, a_out, sems.at[0]),
+        pltpu.make_async_copy(b, b_out, sems.at[1]),
+    ]
+    for copy in copies:
+        copy.start()
+    for copy in copies:
+        copy.wait()
+
+
+def place_call(a, b):
+    vm = pl.BlockSpec(memory_space=pltpu.VMEM)
+    hbm = pl.BlockSpec(memory_space=pltpu.HBM)
+    return pl.pallas_call(
+        place_kernel,
+        out_shape=(jax.ShapeDtypeStruct(a.shape, a.dtype), jax.ShapeDtypeStruct(b.shape, b.dtype)),
+        in_specs=[vm, vm],
+        out_specs=(hbm, hbm),
+        scratch_shapes=[pltpu.SemaphoreType.DMA((2,))],
+        name="place",
+    )(a, b)
 
 
 def local(
@@ -377,11 +425,12 @@
 ):
     del send_count
     fields, score = decoder_call(
-        edge_slot, row_points, processed_latent_nodes[0], w_src,
-        dispatch_node_lookup.reshape(NZ, NX, CAP), gain_node[None, :], channel_weight[None, :],
-        grid_embed, w_dst, w_node, w_out, targets,
+        edge_slot, dispatch_node_lookup.reshape(NZ, NX, CAP),
+        gain_node[None, :], channel_weight[None, :],
+        row_points, processed_latent_nodes[0], w_src, grid_embed, w_dst, w_node, w_out, targets,
     )
-    return fields[None], score[None]
+    fields, score = place_call(fields, score)
+    return fields[None], score.reshape(1, C, G)
 
 
 def solution(mesh):

time: 139 us -> 135 us (0.971)
  local copies, waits for them, and re-layouts: 4.25 us -> 0 us
    unnamed x2 -> x0, local copies, waits for them, and re-layouts: 4.25 us -> none
    pallas_call x0 -> x1, Pallas kernels: none -> 2.12 us  [place_call(): pl.pallas_call(place_kernel, out_shape=(jax.ShapeDtypeStruct(a.shape, a.d...]
    pallas_call x1, Pallas kernels: 133 us -> 131 us  [decoder_call(): pl.pallas_call(decoder_kernel, out_shape=(jax.ShapeDtypeStruct((C, G), ha...]
where the time goes in v4:
time: 135 us
  Pallas kernels  133 us (99%)
  between operations  1.47 us (1%)
    pallas_call x1, Pallas kernels, decoder_call(): pl.pallas_call(decoder_kernel, out_shape=(jax.ShapeDtypeStruct((C, G), ha...  131 us

profile of v4, /device:TPU:1, one launch (start us, length us, event | category | flops | bytes accessed | tf_op | source)
XLA Modules:
  0.0 134.7 jit_solution(14254313121359053)
XLA Ops:
  1.3 131.1 %decoder.1 = (bf16[100,1536]{1,0:T(8,128)(2,1)}, f32[1200,128]{1,0:T(8,128)}) custom-call(s32[3,1536]{1,0:T(4,128)} %edge.1, s32[8,4,128]{2,1,0:T(4,128)} %bitcast.9, f32[1,1024]{1,0:T(1,128)} %bitcast.10, f32[1,100]{1,0:T(1,128)} %bitcast.11, s32[1]{0:T(128)S(6)} %copy.16.rp_hbm, bf16[512,1024]{1,0:T(8,128)(2,1)} %bitcast.6, bf16[1024,1024]{1,0:T(8,128)(2,1)} %wsrc_hbm.1, ...), custom_call_target="tpu_custom_call" | custom-call | flops 14000000000 | bytes 20971520 | tf_op jit(solution)/shard_map/decoder/pallas_call | solution.py:358
  132.4 2.1 %place.1 = (bf16[100,1536]{1,0:T(8,128)(2,1)}, f32[1200,128]{1,0:T(8,128)}) custom-call(bf16[100,1536]{1,0:T(8,128)(2,1)} %get-tuple-element.6.a, f32[1200,128]{1,0:T(8,128)} %get-tuple-element.7.b), custom_call_target="tpu_custom_call" | custom-call | tf_op jit(solution)/shard_map/place/pallas_call | solution.py:412

commit v5 on v4

--- a/solution.py
+++ b/solution.py
@@ -40,7 +40,7 @@
     rp_hbm, latent_hbm, wsrc_hbm, embed_hbm, wdst_hbm, wnode_hbm, wout_hbm, targets_hbm,
     fields_out, score_out,
     T, stage, landing, L, hot, F, gs, S, X,
-    fields_all, rp, latent, w_src, embed, square, w_out, targets,
+    fields_all, order, slots, rp, latent, w_src, embed, square, w_out, targets,
     lk_s, lk_r, z_s, z_r, x_s, x_r, m_s, m_r, pre, first,
 ):
     me = lax.axis_index("rows")
@@ -184,11 +184,17 @@
             pl.semaphore_wait(barrier, len(peers))
         z_copy(0, 1, q).start()
         z_copy(1, 1, q).start()
+        items.append((q, z, q))
+        launch(items[-1], 0)
         if q == 0:
             for k in range(1, NZ):
                 lk_copy(k).start()
-        items.append((q, z, q))
-        launch(items[-1], 0)
+
+    for row in range(G // 32):
+        parts = [edge[k:k + 1, row * 32:(row + 1) * 32] for k in range(K)]
+        order[row:row + 1, :] = jnp.concatenate(parts + [jnp.zeros((1, 32), jnp.int32)], axis=1)
+    load_slots = pltpu.make_async_copy(order, slots, pre.at[7])
+    load_slots.start()
 
     loads[0].wait()
     loads[1].wait()
@@ -229,6 +235,7 @@
     loads[3].wait()
     loads[4].wait()
     load_node.wait()
+    load_slots.wait()
 
     def m_copy(i, b, arriving=False):
         if b == NB - 1:
@@ -273,7 +280,7 @@
                 g = gs[pl.ds(pl.multiple_of(p * 8, 8), 8), :]
                 total = jnp.zeros((8, 128), jnp.float32)
                 for k in range(K):
-                    half = F[edge[k, p]] + g
+                    half = F[slots[start // 32 + q, k * 32 + u]] + g
                     total = total + (half + half * jnp.tanh(half))
                 S[pl.ds(q * 256 + (u // 8) * 64 + u % 8, 8, stride=8), :] = total
 
@@ -351,7 +358,6 @@
 def decoder_call(edge, look, gain, weight, *arrays):
     n_items = Q * NZ
     vm = pl.BlockSpec(memory_space=pltpu.VMEM)
-    sm = pl.BlockSpec(memory_space=pltpu.SMEM)
     hbm = pl.BlockSpec(memory_space=pltpu.HBM)
     dma = pltpu.SemaphoreType.DMA
     half, full = jnp.bfloat16, jnp.float32
@@ -361,7 +367,7 @@
             jax.ShapeDtypeStruct((C, G), half),
             jax.ShapeDtypeStruct((C * (G // 128), 128), full),
         ),
-        in_specs=[sm, vm, vm, vm] + [hbm] * len(arrays),
+        in_specs=[vm, vm, vm, vm] + [hbm] * len(arrays),
         out_specs=(hbm, vm),
         scratch_shapes=[
             pltpu.VMEM((Q, NZ, NODES, W), half),
@@ -374,6 +380,8 @@
             pltpu.VMEM((PB * 8, 128), full),
             pltpu.VMEM((MEMBERS, CP, G), half),
             pltpu.VMEM((C, G), half),
+            pltpu.VMEM((G // 32, 128), jnp.int32),
+            pltpu.SMEM((G // 32, 128), jnp.int32),
             pltpu.SMEM((1,), jnp.int32),
             pltpu.VMEM((NODES, D), half),
             pltpu.VMEM((Q, D, W), half),
@@ -385,7 +393,7 @@
             dma((8 * Q,)), dma((8 * Q,)),
             dma((n_items * 3,)), dma((n_items * 3,)),
             dma((NB * 7,)), dma((NB * 7,)),
-            dma((7,)), dma((Q + 1,)),
+            dma((8,)), dma((Q + 1,)),
         ],
         compiler_params=pltpu.CompilerParams(
             collective_id=0, has_side_effects=True, vmem_limit_bytes=VMEM_LIMIT

time: 135 us -> 132 us (0.978)
  Pallas kernels: 133 us -> 131 us
    pallas_call x1, Pallas kernels: 131 us -> 129 us  [decoder_call(): pl.pallas_call(decoder_kernel, out_shape=(jax.ShapeDtypeStruct((C, G), ha...]
where the time goes in v5:
time: 132 us
  Pallas kernels  131 us (99%)
  between operations  1.47 us (1%)
    pallas_call x1, Pallas kernels, decoder_call(): pl.pallas_call(decoder_kernel, out_shape=(jax.ShapeDtypeStruct((C, G), ha...  129 us

profile of v5, /device:TPU:1, one launch (start us, length us, event | category | flops | bytes accessed | tf_op | source)
XLA Modules:
  0.0 132.1 jit_solution(7519150762413292096)
XLA Ops:
  1.3 128.6 %decoder.1 = (bf16[100,1536]{1,0:T(8,128)(2,1)}, f32[1200,128]{1,0:T(8,128)}) custom-call(s32[3,1536]{1,0:T(4,128)} %edge.1, s32[8,4,128]{2,1,0:T(4,128)} %bitcast.9, f32[1,1024]{1,0:T(1,128)} %bitcast.10, f32[1,100]{1,0:T(1,128)} %bitcast.11, s32[1]{0:T(128)S(6)} %copy.16.rp_hbm, bf16[512,1024]{1,0:T(8,128)(2,1)} %bitcast.6, bf16[1024,1024]{1,0:T(8,128)(2,1)} %wsrc_hbm.1, ...), custom_call_target="tpu_custom_call" | custom-call | flops 14000000000 | bytes 20971520 | tf_op jit(solution)/shard_map/decoder/pallas_call | solution.py:364
  129.8 2.1 %place.1 = (bf16[100,1536]{1,0:T(8,128)(2,1)}, f32[1200,128]{1,0:T(8,128)}) custom-call(bf16[100,1536]{1,0:T(8,128)(2,1)} %get-tuple-element.6.a, f32[1200,128]{1,0:T(8,128)} %get-tuple-element.7.b), custom_call_target="tpu_custom_call" | custom-call | tf_op jit(solution)/shard_map/place/pallas_call | solution.py:420

commit v6 on v5

--- a/solution.py
+++ b/solution.py
@@ -331,14 +331,6 @@
             score_out[pl.ds(tile, C, stride=G // 128), :] = jnp.where(point < limit, wide * total, 0.0)
 
     pass_far(NB - 4)
-    score(0)
-    pass_far(NB - 3)
-    pass_on(NB - 2)
-    score(1)
-    pass_far(NB - 2)
-    for b in range(2, NB):
-        score(b)
-
     for item in items[-SLOTS:]:
         for i in range(NX - 1):
             x_copy(i, item).wait_send()
@@ -349,7 +341,20 @@
                     z_copy(direction, d, q).wait_send()
     for k in range(1, NZ):
         lk_copy(k).wait_send()
-    for b in range(NB):
+    score(0)
+    pass_far(NB - 3)
+    pass_on(NB - 2)
+    score(1)
+    score(2)
+    pass_far(NB - 2)
+    for b in range(3, NB):
+        if b == NB - 1:
+            for done in range(NB - 2):
+                for i in range(7):
+                    m_copy(i, done).wait_send()
+        score(b)
+
+    for b in range(NB - 2, NB):
         for i in range(7):
             m_copy(i, b).wait_send()
     save_fields.wait()

time: 132 us -> 132 us (level)
  no operation moved by 1% of the time
where the time goes in v6:
time: 132 us
  Pallas kernels  131 us (99%)
  between operations  1.47 us (1%)
    pallas_call x1, Pallas kernels, decoder_call(): pl.pallas_call(decoder_kernel, out_shape=(jax.ShapeDtypeStruct((C, G), ha...  128 us

profile of v6, /device:TPU:1, one launch (start us, length us, event | category | flops | bytes accessed | tf_op | source)
XLA Modules:
  0.0 132.0 jit_solution(1513108030954045826)
XLA Ops:
  1.3 128.4 %decoder.1 = (bf16[100,1536]{1,0:T(8,128)(2,1)}, f32[1200,128]{1,0:T(8,128)}) custom-call(s32[3,1536]{1,0:T(4,128)} %edge.1, s32[8,4,128]{2,1,0:T(4,128)} %bitcast.9, f32[1,1024]{1,0:T(1,128)} %bitcast.10, f32[1,100]{1,0:T(1,128)} %bitcast.11, s32[1]{0:T(128)S(6)} %copy.16.rp_hbm, bf16[512,1024]{1,0:T(8,128)(2,1)} %bitcast.6, bf16[1024,1024]{1,0:T(8,128)(2,1)} %wsrc_hbm.1, ...), custom_call_target="tpu_custom_call" | custom-call | flops 14000000000 | bytes 20971520 | tf_op jit(solution)/shard_map/decoder/pallas_call | solution.py:369
  129.7 2.1 %place.1 = (bf16[100,1536]{1,0:T(8,128)(2,1)}, f32[1200,128]{1,0:T(8,128)}) custom-call(bf16[100,1536]{1,0:T(8,128)(2,1)} %get-tuple-element.6.a, f32[1200,128]{1,0:T(8,128)} %get-tuple-element.7.b), custom_call_target="tpu_custom_call" | custom-call | tf_op jit(solution)/shard_map/place/pallas_call | solution.py:425
